TPU v7x, 512 devices: a whole 4x4x16 slice. The times are simulated.
512 devices in a mesh: gx: 16 (over z), gy: 8 (over x, core), sa: 4 (over y).
Axes of the slice: x: 4, y: 4, z: 16, core: 2. Of those that a mesh axis runs over, the one named last changes fastest.
Arguments:
- profile_fields: float32 [32, 4, 524288], P(None, None, ('gx', 'gy', 'sa')), may hold values from -6 to 6
- turbulent_coefficients: float32 [32, 2, 524288], P(None, None, ('gx', 'gy', 'sa')), may hold values from 0.3 to 6
- column_patch_owner: int32 [2, 524288], P(None, ('gx', 'gy', 'sa')), may hold values from 0 to 1023, as said below
- kind_fractions: float32 [6, 524288], P(None, ('gx', 'gy', 'sa')), may hold values from 0.1 to 1
- kind_existing_flags: int32 [5, 524288], P(None, ('gx', 'gy', 'sa')), may hold values 0 or 1
- kind_absorbed_flux: float32 [6, 524288], P(None, ('gx', 'gy', 'sa')), may hold values from -6 to 6
- kind_thermal_links: float32 [6, 524288], P(None, ('gx', 'gy', 'sa')), may hold values from 0.2 to 3
- bottom_kelvin: float32 [6, 524288], P(None, ('gx', 'gy', 'sa')), may hold values from -5 to 5
- drift_speeds: float32 [2, 524288], P(None, ('gx', 'gy', 'sa')), may hold values from -5 to 5
Outputs:
- advanced_profile: float32 [32, 4, 524288], P(None, None, ('gx', 'gy', 'sa'))
- kind_interface_kelvin: float32 [6, 524288], P(None, ('gx', 'gy', 'sa'))
Inputs may be any that keep to these rules, and one draw needn't show every extreme that they name: column_patch_owner[0, i] * 1024 + column_patch_owner[1, i] over all columns i is a permutation of the 524288 cells; row 0 is below 512 and row 1 below 1024. Cell j is held by the device that holds entry j of the cell arrays. The columns of one device have their cells on every device, 1 to 4 of them on each, and exactly 4 on some device.
All inputs are finite; a program needn't handle non-finite values. No bound on the sum of `kind_existing_flags` on one device may be relied on, other than what follows from the above.
Results may differ from a plain program's by a relative error of at most 0.00016.
Values sent between devices are 32-bit elements; how exact they have to be, the bound alone decides.
No kernel may reach another device: no remote copies, remote signals or barrier semaphores. Data moves between devices by JAX's collectives and lax.ppermute only.
A program may use at most 64 MiB of HBM per device.

v0:
```python
import jax
import jax.numpy as jnp
from jax import lax
from jax.sharding import PartitionSpec as P

SWEEPS = 3


VAPOUR_ENTHALPY = 2.5


def vapour_limit(values):
    return 0.6 * jnp.exp(0.3 * values)


def longwave_outgoing(values):
    return 0.5 * jnp.exp(0.2 * values)


def eliminate(values, coupling):

    def eliminate_advance(carried, inputs):
        offset_prev, factor_prev, above_coef = carried
        level_values, below_coef = inputs
        divisor = 1.0 + above_coef * (1.0 - factor_prev) + below_coef
        offset_now = (level_values + above_coef * offset_prev) / divisor
        factor_now = below_coef / divisor
        return ((offset_now, factor_now, below_coef), (offset_now, factor_now))

    zeros_row = jnp.zeros_like(values[0])
    _, (sweep_shifts, sweep_multipliers) = lax.scan(
        eliminate_advance, (zeros_row, zeros_row, zeros_row), (values, coupling)
    )
    return (sweep_shifts, sweep_multipliers)


def substitute(sweep_shifts, sweep_multipliers, boundary):

    def substitute_advance(level_below, inputs):
        level_offset, level_factor = inputs
        solved = level_offset + level_factor * level_below
        return (solved, solved)

    _, solved = lax.scan(
        substitute_advance, boundary, (sweep_shifts, sweep_multipliers), reverse=True
    )
    return solved


def surface_weights(kind_fractions, kind_existing_flags):
    present = jnp.concatenate(
        [jnp.ones_like(kind_existing_flags[:1]), kind_existing_flags], axis=0
    ).astype(jnp.float32)
    unscaled = kind_fractions * present
    return unscaled / jnp.sum(unscaled, axis=0, keepdims=True)


def flux_budget(cell_fields, heat_offset, heat_factor, moist_offset, moist_factor, transfer_factor):
    fraction_shares = cell_fields[0:6]
    absorbed_flux = cell_fields[6:12]
    thermal_link = cell_fields[12:18]
    bottom_layer = cell_fields[18:24]
    interface_kelvin = bottom_layer
    for sweep_index in range(SWEEPS):
        humidity_limit = vapour_limit(interface_kelvin)
        averaged_enthalpy = jnp.sum(fraction_shares * interface_kelvin, axis=0)
        averaged_humidity = jnp.sum(fraction_shares * humidity_limit, axis=0)
        lowest_enthalpy = heat_offset + heat_factor * averaged_enthalpy
        lowest_humidity = moist_offset + moist_factor * averaged_humidity
        outgoing_flux = longwave_outgoing(interface_kelvin)
        budget_residual = (
            absorbed_flux
            - outgoing_flux
            - transfer_factor * (interface_kelvin - lowest_enthalpy)
            - VAPOUR_ENTHALPY * transfer_factor * (humidity_limit - lowest_humidity)
            - thermal_link * (interface_kelvin - bottom_layer)
        )
        budget_slope = (
            0.2 * outgoing_flux
            + transfer_factor * (1.0 + VAPOUR_ENTHALPY * 0.3 * humidity_limit)
            + thermal_link
        )
        interface_kelvin = interface_kelvin + budget_residual / budget_slope
    humidity_limit = vapour_limit(interface_kelvin)
    return (
        interface_kelvin,
        jnp.sum(fraction_shares * interface_kelvin, axis=0),
        jnp.sum(fraction_shares * humidity_limit, axis=0),
    )


def per_device(
    profile_fields,
    turbulent_coefficients,
    column_patch_owner,
    kind_fractions,
    kind_existing_flags,
    kind_absorbed_flux,
    kind_thermal_links,
    bottom_kelvin,
    drift_speeds,
):
    columns = profile_fields.shape[2]
    device_count = lax.axis_size(("gx", "gy", "sa"))
    far_count = lax.axis_size(("gx", "gy"))
    near_count = lax.axis_size("sa")
    capacity = 2 * columns // device_count
    slot_total = device_count * capacity
    owner_dev = column_patch_owner[0]
    local_cell = column_patch_owner[1]
    position = jnp.arange(columns, dtype=jnp.int32)
    sorted_pos = jnp.argsort(owner_dev * columns + position)
    sorted_owner = owner_dev[sorted_pos]
    first_pos = jnp.searchsorted(sorted_owner, sorted_owner, side="left")
    slot_rank = jnp.zeros((columns,), jnp.int32).at[sorted_pos].set(position - first_pos)
    slot_index = owner_dev * capacity + slot_rank
    slot_source = jnp.full((slot_total,), columns, jnp.int32).at[slot_index].set(position)

    def gather_into_parcels(fields):
        padded = jnp.concatenate([fields, jnp.zeros((fields.shape[0], 1), fields.dtype)], axis=1)
        return padded[:, slot_source].reshape(fields.shape[0], far_count, near_count, capacity)

    fraction_shares = surface_weights(kind_fractions, kind_existing_flags)
    patch_directory = jnp.concatenate(
        [fraction_shares, kind_absorbed_flux, kind_thermal_links, bottom_kelvin, drift_speeds],
        axis=0,
    )
    coupling = jnp.repeat(turbulent_coefficients, 2, axis=1)
    cell_code = (local_cell + 1).astype(jnp.float32)
    received = lax.all_to_all(
        lax.all_to_all(
            gather_into_parcels(cell_code[None]),
            ("gx", "gy"),
            split_axis=1,
            concat_axis=1,
            tiled=True,
        ),
        "sa",
        split_axis=2,
        concat_axis=2,
        tiled=True,
    )
    patch_locator = received.reshape(slot_total).astype(jnp.int32) - 1
    served = patch_directory[:, jnp.maximum(patch_locator, 0)].reshape(
        patch_directory.shape[0], far_count, near_count, capacity
    )
    buffer = lax.all_to_all(
        lax.all_to_all(served, ("gx", "gy"), split_axis=1, concat_axis=1, tiled=True),
        "sa",
        split_axis=2,
        concat_axis=2,
        tiled=True,
    )
    gathered_fields = buffer.reshape(buffer.shape[0], slot_total)[:, slot_index]
    sweep_shifts, sweep_multipliers = eliminate(profile_fields, coupling)
    interface_kelvin, averaged_enthalpy, averaged_humidity = flux_budget(
        gathered_fields,
        sweep_shifts[-1, 0],
        sweep_multipliers[-1, 0],
        sweep_shifts[-1, 1],
        sweep_multipliers[-1, 1],
        turbulent_coefficients[-1, 0],
    )
    arrived = lax.all_to_all(
        lax.all_to_all(
            gather_into_parcels(interface_kelvin),
            ("gx", "gy"),
            split_axis=1,
            concat_axis=1,
            tiled=True,
        ),
        "sa",
        split_axis=2,
        concat_axis=2,
        tiled=True,
    )
    target = jnp.where(patch_locator >= 0, patch_locator, columns)
    slot_ids = jnp.arange(slot_total, dtype=jnp.int32)
    kind_interface_kelvin = arrived.reshape(6, slot_total)[
        :, jnp.zeros((columns,), jnp.int32).at[target].set(slot_ids, mode="drop")
    ]
    boundary = jnp.stack(
        [averaged_enthalpy, averaged_humidity, gathered_fields[24], gathered_fields[25]], axis=0
    )
    advanced_profile = substitute(sweep_shifts, sweep_multipliers, boundary)
    return (advanced_profile, kind_interface_kelvin)


def solution(mesh):
    in_specs = (
        P(None, None, ("gx", "gy", "sa")),
        P(None, None, ("gx", "gy", "sa")),
        P(None, ("gx", "gy", "sa")),
        P(None, ("gx", "gy", "sa")),
        P(None, ("gx", "gy", "sa")),
        P(None, ("gx", "gy", "sa")),
        P(None, ("gx", "gy", "sa")),
        P(None, ("gx", "gy", "sa")),
        P(None, ("gx", "gy", "sa")),
    )
    out_specs = (P(None, None, ("gx", "gy", "sa")), P(None, ("gx", "gy", "sa")))
    return jax.shard_map(
        per_device, mesh=mesh, in_specs=in_specs, out_specs=out_specs, check_vma=False
    )
```

profile of v0, /device:TPU:6, one launch (start us, length us, event | category | flops | bytes accessed | tf_op | source)
XLA Modules:
  0.0 293.0 jit_solution(10097094405320051286)
XLA Ops:
  1.5 4.4 %sort.17 = (s32[1024]{0:T(1024)}, s32[1024]{0:T(1024)S(1)}) sort(s32[1024]{0:T(1024)S(1)} %iota_add_fusion, s32[1024]{0:T(1024)S(1)} %iota.15), dimensions={0}, to_apply=%region_1.2 | sort | flops 10240 | bytes 16384 | tf_op jit(solution)/shard_map/jit(argsort)/sort | solution.py:112
  5.8 4.5 %gather_fusion.1 = s32[1024]{0:T(1024)S(1)} fusion(s32[1024]{0:T(1024)S(1)} %bitcast.52, s32[1024]{0:T(1024)S(1)} %get-tuple-element.349), kind=kCustom, calls=%fused_computation.1 | custom fusion | bytes 12288 | tf_op jit(solution)/shard_map/gather | solution.py:113
  10.4 50.7 %while.61 = (s32[]{:T(128)}, u32[1024]{0:T(1024)S(1)}, u32[1024]{0:T(1024)S(1)}, s32[1024]{0:T(1024)S(1)}, s32[]{:T(128)}, /*index=5*/s32[]{:T(128)}, s32[]{}) while((s32[]{:T(128)}, u32[1024]{0:T(1024)S(1)}, u32[1024]{0:T(1024)S(1)}, s32[1024]{0:T(1024)S(1)}, s32[]{:T(128)}, /*index=5*/s32[]{:T(128)}, s32[]{}) %tuple.119), condition=%wide.region_3.4_spmd.clone, body=%wide.region_2.3_spmd.clone.sunk | while | flops 19460 | bytes 67693 | solution.py:114
  10.4 4.5 %gather_fusion = s32[1024]{0:T(1024)S(1)} fusion(s32[1024]{0:T(1024)S(1)} %get-tuple-element.493, u32[1024]{0:T(1024)S(1)} %broadcast_clamp_fusion.5), kind=kCustom, calls=%fused_computation.clone.clone.1 | custom fusion | bytes 12288 | tf_op jit(solution)/shard_map/jit(searchsorted)/jit(_searchsorted_scan_impl)/vmap(jit(_searchsorted_scan_impl))/while/body/eval_jaxpr/gather | solution.py:114
  15.0 4.5 %gather_fusion = s32[1024]{0:T(1024)S(1)} fusion(s32[1024]{0:T(1024)S(1)} %get-tuple-element.493, u32[1024]{0:T(1024)S(1)} %broadcast_clamp_fusion.5), kind=kCustom, calls=%fused_computation.clone.clone.1 | custom fusion | bytes 12288 | tf_op jit(solution)/shard_map/jit(searchsorted)/jit(_searchsorted_scan_impl)/vmap(jit(_searchsorted_scan_impl))/while/body/eval_jaxpr/gather | solution.py:114
  19.6 4.5 %gather_fusion = s32[1024]{0:T(1024)S(1)} fusion(s32[1024]{0:T(1024)S(1)} %get-tuple-element.493, u32[1024]{0:T(1024)S(1)} %broadcast_clamp_fusion.5), kind=kCustom, calls=%fused_computation.clone.clone.1 | custom fusion | bytes 12288 | tf_op jit(solution)/shard_map/jit(searchsorted)/jit(_searchsorted_scan_impl)/vmap(jit(_searchsorted_scan_impl))/while/body/eval_jaxpr/gather | solution.py:114
  24.2 4.5 %gather_fusion = s32[1024]{0:T(1024)S(1)} fusion(s32[1024]{0:T(1024)S(1)} %get-tuple-element.493, u32[1024]{0:T(1024)S(1)} %broadcast_clamp_fusion.5), kind=kCustom, calls=%fused_computation.clone.clone.1 | custom fusion | bytes 12288 | tf_op jit(solution)/shard_map/jit(searchsorted)/jit(_searchsorted_scan_impl)/vmap(jit(_searchsorted_scan_impl))/while/body/eval_jaxpr/gather | solution.py:114
  28.8 4.5 %gather_fusion = s32[1024]{0:T(1024)S(1)} fusion(s32[1024]{0:T(1024)S(1)} %get-tuple-element.493, u32[1024]{0:T(1024)S(1)} %broadcast_clamp_fusion.5), kind=kCustom, calls=%fused_computation.clone.clone.1 | custom fusion | bytes 12288 | tf_op jit(solution)/shard_map/jit(searchsorted)/jit(_searchsorted_scan_impl)/vmap(jit(_searchsorted_scan_impl))/while/body/eval_jaxpr/gather | solution.py:114
  33.4 4.5 %gather_fusion = s32[1024]{0:T(1024)S(1)} fusion(s32[1024]{0:T(1024)S(1)} %get-tuple-element.493, u32[1024]{0:T(1024)S(1)} %broadcast_clamp_fusion.5), kind=kCustom, calls=%fused_computation.clone.clone.1 | custom fusion | bytes 12288 | tf_op jit(solution)/shard_map/jit(searchsorted)/jit(_searchsorted_scan_impl)/vmap(jit(_searchsorted_scan_impl))/while/body/eval_jaxpr/gather | solution.py:114
  38.1 4.5 %gather_fusion = s32[1024]{0:T(1024)S(1)} fusion(s32[1024]{0:T(1024)S(1)} %get-tuple-element.493, u32[1024]{0:T(1024)S(1)} %broadcast_clamp_fusion.5), kind=kCustom, calls=%fused_computation.clone.clone.1 | custom fusion | bytes 12288 | tf_op jit(solution)/shard_map/jit(searchsorted)/jit(_searchsorted_scan_impl)/vmap(jit(_searchsorted_scan_impl))/while/body/eval_jaxpr/gather | solution.py:114
  42.7 4.5 %gather_fusion = s32[1024]{0:T(1024)S(1)} fusion(s32[1024]{0:T(1024)S(1)} %get-tuple-element.493, u32[1024]{0:T(1024)S(1)} %broadcast_clamp_fusion.5), kind=kCustom, calls=%fused_computation.clone.clone.1 | custom fusion | bytes 12288 | tf_op jit(solution)/shard_map/jit(searchsorted)/jit(_searchsorted_scan_impl)/vmap(jit(_searchsorted_scan_impl))/while/body/eval_jaxpr/gather | solution.py:114
  47.3 4.5 %gather_fusion = s32[1024]{0:T(1024)S(1)} fusion(s32[1024]{0:T(1024)S(1)} %get-tuple-element.493, u32[1024]{0:T(1024)S(1)} %broadcast_clamp_fusion.5), kind=kCustom, calls=%fused_computation.clone.clone.1 | custom fusion | bytes 12288 | tf_op jit(solution)/shard_map/jit(searchsorted)/jit(_searchsorted_scan_impl)/vmap(jit(_searchsorted_scan_impl))/while/body/eval_jaxpr/gather | solution.py:114
  51.9 4.5 %gather_fusion = s32[1024]{0:T(1024)S(1)} fusion(s32[1024]{0:T(1024)S(1)} %get-tuple-element.493, u32[1024]{0:T(1024)S(1)} %broadcast_clamp_fusion.5), kind=kCustom, calls=%fused_computation.clone.clone.1 | custom fusion | bytes 12288 | tf_op jit(solution)/shard_map/jit(searchsorted)/jit(_searchsorted_scan_impl)/vmap(jit(_searchsorted_scan_impl))/while/body/eval_jaxpr/gather | solution.py:114
  56.5 4.5 %gather_fusion = s32[1024]{0:T(1024)S(1)} fusion(s32[1024]{0:T(1024)S(1)} %get-tuple-element.493, u32[1024]{0:T(1024)S(1)} %broadcast_clamp_fusion.5), kind=kCustom, calls=%fused_computation.clone.clone.1 | custom fusion | bytes 12288 | tf_op jit(solution)/shard_map/jit(searchsorted)/jit(_searchsorted_scan_impl)/vmap(jit(_searchsorted_scan_impl))/while/body/eval_jaxpr/gather | solution.py:114
  61.1 4.3 %scatter_custom_fusion = s32[1024]{0:T(1024)S(1)} fusion(s32[1024]{0:T(1024)S(1)} %get-tuple-element.350, s32[1024]{0:T(1024)S(1)} %convert_subtract_fusion, s32[]{:T(128)} %copy.113), kind=kCustom, calls=%fused_computation.77 | custom fusion | bytes 4100 | tf_op jit(solution)/shard_map/scatter | solution.py:115
  66.0 4.3 %scatter_custom_fusion.1 = s32[2048]{0:T(1024)S(1)} fusion(s32[1024]{0:T(1024)S(1)} %get-tuple-element.340, s32[1024]{0:T(1024)S(1)} %iota.17, s32[]{:T(128)} %constant.116.clone.1), kind=kCustom, calls=%fused_computation.69 | custom fusion | bytes 8196 | tf_op jit(solution)/shard_map/scatter | solution.py:117
  70.4 11.8 %gather_fusion.2 = f32[2048]{0:T(1024)S(1)} fusion(f32[1025]{0:T(1024)S(1)} %maximum_reduce_fusion, s32[2048]{0:T(1024)S(1)} %fusion.10), kind=kCustom, calls=%fused_computation.2 | custom fusion | bytes 24576 | tf_op jit(solution)/shard_map/gather | solution.py:121
  83.3 19.5 %all-to-all-start = ((f32[1,128,4,4]{3,2,0,1:T(4,128)}), f32[1,128,4,4]{3,2,0,1:T(4,128)S(1)}, u32[]{:S(2)}, u32[]{:S(2)}) async-start(f32[1,128,4,4]{3,2,0,1:T(4,128)} %bitcast.4), calls=%async_computation | async-start | bytes 524288 | tf_op jit(solution)/shard_map/all_to_all | solution.py:131
  102.8 21.9 %all-to-all-done = f32[1,128,4,4]{3,2,0,1:T(4,128)S(1)} async-done(((f32[1,128,4,4]{3,2,0,1:T(4,128)}), f32[1,128,4,4]{3,2,0,1:T(4,128)S(1)}, u32[]{:S(2)}, u32[]{:S(2)}) %all-to-all-start) | async-done | bytes 8224 | tf_op jit(solution)/shard_map/all_to_all | solution.py:131
  125.4 4.5 %all-to-all-start.1 = ((f32[1,128,4,4]{1,3,0,2:T(4,128)}), f32[1,128,4,4]{1,3,0,2:T(4,128)S(1)}, u32[]{:S(2)}, u32[]{:S(2)}) async-start(f32[1,128,4,4]{1,3,0,2:T(4,128)} %copy.62), calls=%async_computation.1 | async-start | bytes 16384 | tf_op jit(solution)/shard_map/all_to_all | solution.py:130
  136.3 5.5 %gather_fusion.3 = f32[2048,26]{1,0:T(8,128)S(1)} fusion(f32[26,1024]{0,1:T(8,128)S(1)} %copy.64, s32[2048]{0:T(1024)S(1)} %broadcast_clamp_fusion.1), kind=kCustom, calls=%fused_computation.3 | custom fusion | bytes 434176 | tf_op jit(solution)/shard_map/gather | solution.py:144
  144.4 6.9 %all-to-all-start.2 = ((f32[128,1,416]{2,1,0:T(1,128)}), f32[128,1,416]{2,1,0:T(1,128)S(1)}, u32[]{:S(2)}, u32[]{:S(2)}) async-start(f32[128,1,416]{2,1,0:T(1,128)} %reshape.247), calls=%async_computation.2 | async-start | bytes 524288 | tf_op jit(solution)/shard_map/all_to_all | solution.py:148
  151.5 26.4 %while.62 = (s32[]{:T(128)}, f32[4,1024]{1,0:T(4,128)S(1)}, f32[4,1024]{1,0:T(4,128)S(1)}, f32[4,1024]{1,0:T(4,128)S(1)}, f32[32,4,1024]{2,1,0:T(4,128)S(1)}, /*...) while((s32[]{:T(128)}, f32[4,1024]{1,0:T(4,128)S(1)}, ...), condition=%wide.region_7.8_spmd.clone, body=%wide.region_6.7_spmd.clone.sunk | while | flops 61443 | bytes 278656 | solution.py:31
  182.5 3.4 %all-to-all-start.3 = ((f32[26,128,4,4]{1,3,0,2:T(4,128)}), f32[26,128,4,4]{1,3,0,2:T(4,128)S(1)}, u32[]{:S(2)}, u32[]{:S(2)}) async-start(f32[26,128,4,4]{1,3,0,2:T(4,128)} %copy.65), calls=%async_computation.3 | async-start | bytes 425984 | tf_op jit(solution)/shard_map/all_to_all | solution.py:147
  185.9 8.2 %scatter_custom_fusion.2 = s32[1024]{0:T(1024)S(1)} fusion(s32[2048]{0:T(1024)} %bitcast.83, s32[2048]{0:T(1024)S(1)} %iota.18, s32[]{:T(128)} %copy.113), kind=kCustom, calls=%fused_computation.75 | custom fusion | bytes 4608 | tf_op jit(solution)/shard_map/scatter | solution.py:180
  194.8 2.8 gather_fusion.4
  199.1 7.6 %gather_fusion.5 = f32[2048,6]{1,0:T(8,128)} fusion(f32[6,1025]{0,1:T(8,128)S(1)} %concatenate.15.clone, s32[2048]{0:T(1024)S(1)} %copy-done.5), kind=kCustom, calls=%fused_computation.5 | custom fusion | bytes 106496 | tf_op jit(solution)/shard_map/gather | solution.py:121
  206.7 16.1 %all-to-all-start.4 = ((f32[6,128,4,4]{0,3,2,1:T(4,128)}), f32[6,128,4,4]{0,3,2,1:T(4,128)S(1)}, u32[]{:S(2)}, u32[]{:S(2)}) async-start(f32[6,128,4,4]{0,3,2,1:T(4,128)} %bitcast.18), calls=%async_computation.4 | async-start | bytes 2097152 | tf_op jit(solution)/shard_map/all_to_all | solution.py:165
  222.8 54.5 %all-to-all-done.4 = f32[6,128,4,4]{0,3,2,1:T(4,128)S(1)} async-done(((f32[6,128,4,4]{0,3,2,1:T(4,128)}), f32[6,128,4,4]{0,3,2,1:T(4,128)S(1)}, u32[]{:S(2)}, u32[]{:S(2)}) %all-to-all-start.4) | async-done | bytes 49184 | tf_op jit(solution)/shard_map/all_to_all | solution.py:165
  278.5 4.7 %all-to-all-start.5 = ((f32[6,128,4,4]{1,3,0,2:T(4,128)}), f32[6,128,4,4]{1,3,0,2:T(4,128)S(1)}, u32[]{:S(2)}, u32[]{:S(2)}) async-start(f32[6,128,4,4]{1,3,0,2:T(4,128)} %copy.69), calls=%async_computation.5 | async-start | bytes 98304 | tf_op jit(solution)/shard_map/all_to_all | solution.py:164
  284.8 4.0 %all-to-all-done.5 = f32[6,128,4,4]{1,3,0,2:T(4,128)S(1)} async-done(((f32[6,128,4,4]{1,3,0,2:T(4,128)}), f32[6,128,4,4]{1,3,0,2:T(4,128)S(1)}, u32[]{:S(2)}, u32[]{:S(2)}) %all-to-all-start.5) | async-done | bytes 49184 | tf_op jit(solution)/shard_map/all_to_all | solution.py:164
  289.4 2.8 gather_fusion.6
  (289 shorter events, 49.5 us)
Async XLA Ops:
  70.4 11.8 %copy-start.4 = (s32[2048]{0:T(1024)}, s32[2048]{0:T(1024)S(1)}, u32[]{:S(2)}) copy-start(s32[2048]{0:T(1024)S(1)} %fusion.10) | copy-start | bytes 24580
  83.3 19.5 %copy-start.2 = (f32[6,1024]{1,0:T(8,128)S(1)}, f32[6,1024]{1,0:T(8,128)}, u32[]{:S(2)}) copy-start(f32[6,1024]{1,0:T(8,128)} %param.18) | copy-start | bytes 73732
  83.3 19.5 %copy-start.3 = (s32[5,1024]{1,0:T(8,128)S(1)}, s32[5,1024]{1,0:T(8,128)}, u32[]{:S(2)}) copy-start(s32[5,1024]{1,0:T(8,128)} %param.19) | copy-start | bytes 61444
  83.3 41.4 %all-to-all-start = ((f32[1,128,4,4]{3,2,0,1:T(4,128)}), f32[1,128,4,4]{3,2,0,1:T(4,128)S(1)}, u32[]{:S(2)}, u32[]{:S(2)}) async-start(f32[1,128,4,4]{3,2,0,1:T(4,128)} %bitcast.4), calls=%async_computation | async-start | bytes 524288 | tf_op jit(solution)/shard_map/all_to_all | solution.py:131
  125.4 9.8 %all-to-all-start.1 = ((f32[1,128,4,4]{1,3,0,2:T(4,128)}), f32[1,128,4,4]{1,3,0,2:T(4,128)S(1)}, u32[]{:S(2)}, u32[]{:S(2)}) async-start(f32[1,128,4,4]{1,3,0,2:T(4,128)} %copy.62), calls=%async_computation.1 | async-start | bytes 16384 | tf_op jit(solution)/shard_map/all_to_all | solution.py:130
  129.9 0.8 copy-start.6
  129.9 0.8 copy-start.7
  129.9 0.8 copy-start.8
  129.9 0.8 copy-start.10
  130.9 1.0 copy-start.1
  144.4 33.6 %all-to-all-start.2 = ((f32[128,1,416]{2,1,0:T(1,128)}), f32[128,1,416]{2,1,0:T(1,128)S(1)}, u32[]{:S(2)}, u32[]{:S(2)}) async-start(f32[128,1,416]{2,1,0:T(1,128)} %reshape.247), calls=%async_computation.2 | async-start | bytes 524288 | tf_op jit(solution)/shard_map/all_to_all | solution.py:148
  182.5 11.6 %all-to-all-start.3 = ((f32[26,128,4,4]{1,3,0,2:T(4,128)}), f32[26,128,4,4]{1,3,0,2:T(4,128)S(1)}, u32[]{:S(2)}, u32[]{:S(2)}) async-start(f32[26,128,4,4]{1,3,0,2:T(4,128)} %copy.65), calls=%async_computation.3 | async-start | bytes 425984 | tf_op jit(solution)/shard_map/all_to_all | solution.py:147
  194.1 0.7 copy-start.9
  198.4 0.7 copy-start.5
  206.7 70.7 %all-to-all-start.4 = ((f32[6,128,4,4]{0,3,2,1:T(4,128)}), f32[6,128,4,4]{0,3,2,1:T(4,128)S(1)}, u32[]{:S(2)}, u32[]{:S(2)}) async-start(f32[6,128,4,4]{0,3,2,1:T(4,128)} %bitcast.18), calls=%async_computation.4 | async-start | bytes 2097152 | tf_op jit(solution)/shard_map/all_to_all | solution.py:165
  278.5 10.3 %all-to-all-start.5 = ((f32[6,128,4,4]{1,3,0,2:T(4,128)}), f32[6,128,4,4]{1,3,0,2:T(4,128)S(1)}, u32[]{:S(2)}, u32[]{:S(2)}) async-start(f32[6,128,4,4]{1,3,0,2:T(4,128)} %copy.69), calls=%async_computation.5 | async-start | bytes 98304 | tf_op jit(solution)/shard_map/all_to_all | solution.py:164
  284.7 4.7 %copy-start = (f32[32,4,1024]{2,1,0:T(4,128)}, f32[32,4,1024]{2,1,0:T(4,128)S(1)}, u32[]{:S(2)}) copy-start(f32[32,4,1024]{2,1,0:T(4,128)S(1)} %get-tuple-element.283) | copy-start | bytes 1572868
where the time goes:
time: 297 us; the launch traced here: 293 us
  local copies, waits for them, and re-layouts  117 us (39%)
  waiting for transfers between devices  82.9 us (28%)
  starting transfers between devices  55.1 us (19%)
  other arithmetic  34.2 us (12%)
    all_to_all x1, waiting for transfers between devices, per_device(): lax.all_to_all(gather_into_parcels(interface_kelvin), ('gx', 'gy'), split...  54.5 us
    gather x11, local copies, waits for them, and re-layouts, per_device(): first_pos = jnp.searchsorted(sorted_owner, sorted_owner, side='left')  49.8 us
    dynamic_update_slice x96, other arithmetic, eliminate(): lax.scan(eliminate_advance, (zeros_row, zeros_row, zeros_row), (values, c...  25.9 us
    all_to_all x1, waiting for transfers between devices, per_device(): lax.all_to_all(gather_into_parcels(cell_code[None]), ('gx', 'gy'), split_...  21.9 us
    all_to_all x1, starting transfers between devices, per_device(): lax.all_to_all(gather_into_parcels(cell_code[None]), ('gx', 'gy'), split_...  19.5 us
    gather x2, local copies, waits for them, and re-layouts, gather_into_parcels(): padded[:, slot_source]  19.4 us
    all_to_all x1, starting transfers between devices, per_device(): lax.all_to_all(gather_into_parcels(interface_kelvin), ('gx', 'gy'), split...  16.1 us
    scatter x1, local copies, waits for them, and re-layouts, per_device(): jnp.zeros((columns,), jnp.int32).at[target].set(slot_ids, mode='drop')  8.18 us
  transfers between devices with their start and end apart: 6, of which 4 were waited for; matrix products, arithmetic and copies ran while one was open for 12% of the time, Pallas kernels for 0%

commit v1 on v0

v1 whole, which is shorter than its diff:
```python
import jax
import jax.numpy as jnp
from jax import lax
from jax.experimental import pallas as pl
from jax.experimental.pallas import tpu as pltpu
from jax.sharding import PartitionSpec as P

SWEEPS = 3
WORDS = 8
CAP = 4
LANES = 128
VAPOUR_ENTHALPY = 2.5
NT = (((1,), (1,)), ((), ()))
NN = (((1,), (0,)), ((), ()))


def halves(x):
    high = x.astype(jnp.bfloat16)
    return high, (x - high.astype(jnp.float32)).astype(jnp.bfloat16)


def one_hot(index_row, count):
    ids = lax.broadcasted_iota(jnp.int32, (count, index_row.shape[1]), 0)
    return jnp.where(ids == index_row, 1.0, 0.0).astype(jnp.bfloat16)


def dot(a, b, dims):
    return lax.dot_general(a, b, dims, preferred_element_type=jnp.float32)


def columns_kernel(far, near, prof_ref, coef_ref, owner_ref, off_ref, fac_ref, send_ref, slot_ref):
    levels, fields, n = prof_ref.shape
    scalar_row = lax.broadcasted_iota(jnp.int32, (fields, n), 0) < 2
    owner = owner_ref[0:1, :]
    blocks = n // LANES
    tall = jnp.concatenate([owner[:, j * LANES:(j + 1) * LANES] for j in range(blocks)], axis=0).T
    earlier = lax.broadcasted_iota(jnp.int32, (LANES, LANES), 0) < lax.broadcasted_iota(jnp.int32, (LANES, LANES), 1)
    totals = [jnp.zeros((1, LANES), jnp.int32) for _ in range(blocks)]
    for i in range(blocks):
        source = jnp.broadcast_to(tall[:, i:i + 1], (LANES, LANES))
        for j in range(i, blocks):
            same = source == owner[:, j * LANES:(j + 1) * LANES]
            if i == j:
                same = same & earlier
            totals[j] += jnp.sum(same.astype(jnp.int32), axis=0, keepdims=True)
    slot = owner * CAP + jnp.concatenate(totals, axis=1)
    slot_ref[...] = slot

    above = factor = offset = jnp.zeros((fields, n), jnp.float32)
    for k in range(levels):
        below = jnp.where(scalar_row, coef_ref[k, 0:1, :], coef_ref[k, 1:2, :])
        inverse = 1.0 / (1.0 + above * (1.0 - factor) + below)
        offset = (prof_ref[k] + above * offset) * inverse
        factor = below * inverse
        above = below
        off_ref[k] = offset
        fac_ref[k] = factor

    values = jnp.concatenate(
        [
            (owner_ref[1:2, :] + 1).astype(jnp.float32),
            offset[0:2],
            factor[0:1],
            above[0:1],
            jnp.zeros((WORDS - 5, n), jnp.float32),
        ],
        axis=0,
    )
    per_far = near * CAP
    row = slot // per_far
    spread = jnp.concatenate([jnp.where(row == g, values, 0.0) for g in range(far)], axis=0)
    place = one_hot(slot % per_far, per_far)
    sent = dot(jnp.concatenate(halves(spread), axis=0), place, NT)
    rows = far * WORDS
    send_ref[...] = (sent[:rows] + sent[rows:]).reshape(far, WORDS, per_far)


def cells_kernel(got_ref, share_ref, flux_ref, link_ref, bottom_ref, drift_ref, kelvin_ref, reply_ref):
    far = reply_ref.shape[0]
    per_far = reply_ref.shape[2]
    n = share_ref.shape[1]
    blocks = n // LANES
    got = got_ref[...].reshape(per_far, far * WORDS).T
    got = jnp.concatenate([got[g * WORDS:(g + 1) * WORDS] for g in range(far)], axis=1)
    cell = got[0:1].astype(jnp.int32) - 1
    block = cell // LANES
    block = jnp.where(cell < 0, -1, block)
    place = one_hot(cell % LANES, LANES)
    spread = jnp.concatenate([jnp.where(block == b, got, 0.0) for b in range(blocks)], axis=0)
    rows = blocks * WORDS
    held = dot(jnp.concatenate(halves(spread), axis=0), place, NT)
    held = held[:rows] + held[rows:]
    held = jnp.concatenate([held[b * WORDS:(b + 1) * WORDS] for b in range(blocks)], axis=1)
    heat_offset, moist_offset, factor, exchange = (held[k:k + 1] for k in range(1, 5))

    share, flux, link, bottom = share_ref[...], flux_ref[...], link_ref[...], bottom_ref[...]
    temp = bottom
    for _ in range(SWEEPS):
        sat = 0.6 * jnp.exp(0.3 * temp)
        air_heat = heat_offset + factor * jnp.sum(share * temp, axis=0, keepdims=True)
        air_moist = moist_offset + factor * jnp.sum(share * sat, axis=0, keepdims=True)
        emitted = 0.5 * jnp.exp(0.2 * temp)
        residual = (
            flux
            - emitted
            - exchange * (temp - air_heat)
            - VAPOUR_ENTHALPY * exchange * (sat - air_moist)
            - link * (temp - bottom)
        )
        slope = 0.2 * emitted + exchange * (1.0 + VAPOUR_ENTHALPY * 0.3 * sat) + link
        temp = temp + residual / slope
    kelvin_ref[...] = temp
    answer = jnp.concatenate(
        [
            jnp.sum(share * temp, axis=0, keepdims=True),
            jnp.sum(share * (0.6 * jnp.exp(0.3 * temp)), axis=0, keepdims=True),
            drift_ref[...],
            jnp.zeros((WORDS - 4, n), jnp.float32),
        ],
        axis=0,
    )
    answer = jnp.concatenate([answer[:, b * LANES:(b + 1) * LANES] for b in range(blocks)], axis=0)
    spread = dot(jnp.concatenate(halves(answer), axis=1), jnp.concatenate([place, place], axis=0), NN)
    reply = jnp.zeros((WORDS, far * per_far), jnp.float32)
    for b in range(blocks):
        reply = reply + jnp.where(block == b, spread[b * WORDS:(b + 1) * WORDS], 0.0)
    for g in range(far):
        reply_ref[g] = reply[:, g * per_far:(g + 1) * per_far]


def finish_kernel(back_ref, slot_ref, off_ref, fac_ref, out_ref):
    levels, fields, n = off_ref.shape
    near, cap, width = back_ref.shape
    per_far = near * cap
    far = width // WORDS
    slot = slot_ref[...]
    row = slot // per_far
    place = one_hot(slot % per_far, per_far)
    back = back_ref[...].reshape(per_far, width).T
    spread = dot(jnp.concatenate(halves(back), axis=1), jnp.concatenate([place, place], axis=0), NN)
    level = jnp.zeros((WORDS, n), jnp.float32)
    for g in range(far):
        level = level + jnp.where(row == g, spread[g * WORDS:(g + 1) * WORDS], 0.0)
    level = level[0:fields]
    for k in range(levels - 1, -1, -1):
        level = off_ref[k] + fac_ref[k] * level
        out_ref[k] = level


def call(kernel, out_shape, *args):
    vmem = pl.BlockSpec(memory_space=pltpu.VMEM)
    return pl.pallas_call(
        kernel,
        out_shape=out_shape,
        in_specs=[vmem] * len(args),
        out_specs=jax.tree.map(lambda _: vmem, out_shape),
        compiler_params=pltpu.CompilerParams(vmem_limit_bytes=40 * 1024 * 1024),
    )(*args)


def surface_weights(kind_fractions, kind_existing_flags):
    present = jnp.concatenate(
        [jnp.ones_like(kind_existing_flags[:1]), kind_existing_flags], axis=0
    ).astype(jnp.float32)
    unscaled = kind_fractions * present
    return unscaled / jnp.sum(unscaled, axis=0, keepdims=True)


def exchange_parcels(parcels, near):
    far = parcels.shape[0]
    parcels = lax.all_to_all(parcels, "gx", split_axis=0, concat_axis=0, tiled=True)
    parcels = parcels.reshape(far * WORDS, near * CAP).T.reshape(near, CAP, far * WORDS)
    return lax.all_to_all(parcels, ("gy", "sa"), split_axis=0, concat_axis=0, tiled=True)


def per_device(profile, coefficients, owner, fractions, flags, flux, links, bottom, drift):
    far = lax.axis_size("gx")
    near = lax.axis_size(("gy", "sa"))
    n = profile.shape[2]
    f32 = jnp.float32
    shape = jax.ShapeDtypeStruct
    share = surface_weights(fractions, flags)
    parcels = shape((far, WORDS, near * CAP), f32)
    offsets, factors, send, slot = call(
        lambda *refs: columns_kernel(far, near, *refs),
        (shape(profile.shape, f32), shape(profile.shape, f32), parcels, shape((1, n), jnp.int32)),
        profile, coefficients, owner,
    )
    got = exchange_parcels(send, near)
    kelvin, reply = call(
        cells_kernel, (shape(bottom.shape, f32), parcels), got, share, flux, links, bottom, drift
    )
    back = exchange_parcels(reply, near)
    advanced = call(finish_kernel, shape(profile.shape, f32), back, slot, offsets, factors)
    return advanced, kelvin


def solution(mesh):
    spread3 = P(None, None, ("gx", "gy", "sa"))
    spread2 = P(None, ("gx", "gy", "sa"))
    return jax.shard_map(
        per_device,
        mesh=mesh,
        in_specs=(spread3, spread3) + (spread2,) * 7,
        out_specs=(spread3, spread2),
        check_vma=False,
    )
```

time: 297 us -> 79.3 us (0.27)
  the two profiles are of different devices: /device:TPU:6 before, /device:TPU:1 now
where the time goes in v1:
time: 79.3 us; the launch traced here: 78.8 us
  blocking collectives  26.5 us (33%)
  starting transfers between devices  25.2 us (32%)
  waiting for transfers between devices  18.7 us (24%)
  Pallas kernels  4.15 us (5%)
  local copies, waits for them, and re-layouts  3.53 us (4%)
    all_to_all x1, starting transfers between devices, exchange_parcels(): lax.all_to_all(parcels, 'gx', split_axis=0, concat_axis=0, tiled=True)  15.9 us
    all_to_all x1, blocking collectives, exchange_parcels(): lax.all_to_all(parcels, 'gx', split_axis=0, concat_axis=0, tiled=True)  14.3 us
    all_to_all x1, blocking collectives, exchange_parcels(): lax.all_to_all(parcels, ('gy', 'sa'), split_axis=0, concat_axis=0, tiled=...  12.2 us
    all_to_all x1, waiting for transfers between devices, exchange_parcels(): lax.all_to_all(parcels, 'gx', split_axis=0, concat_axis=0, tiled=True)  11.5 us
    all_to_all x1, starting transfers between devices, exchange_parcels(): lax.all_to_all(parcels, ('gy', 'sa'), split_axis=0, concat_axis=0, tiled=...  9.33 us
    all_to_all x1, waiting for transfers between devices, exchange_parcels(): lax.all_to_all(parcels, ('gy', 'sa'), split_axis=0, concat_axis=0, tiled=...  7.21 us
    pallas_call x3, Pallas kernels, call(): pl.pallas_call(kernel, out_shape=out_shape, in_specs=[vmem] * len(args),...  4.15 us
    unnamed x18, local copies, waits for them, and re-layouts  2.71 us
  transfers between devices with their start and end apart: 2, of which 2 were waited for; matrix products, arithmetic and copies ran while one was open for 0% of the time, Pallas kernels for 0%

profile of v1, /device:TPU:1, one launch (start us, length us, event | category | flops | bytes accessed | tf_op | source)
XLA Modules:
  0.0 78.8 jit_solution(12139151079892189477)
XLA Ops:
  0.6 0.0 copy-start
  0.6 1.0 %copy-done = f32[32,4,1024]{2,1,0:T(4,128)S(1)} copy-done((f32[32,4,1024]{2,1,0:T(4,128)S(1)}, f32[32,4,1024]{2,1,0:T(4,128)}, u32[]{:S(2)}) %copy-start) | copy-done | bytes 524312
  1.7 0.0 copy-start.1
  1.7 0.9 %copy-done.1 = f32[32,2,1024]{2,1,0:T(2,128)S(1)} copy-done((f32[32,2,1024]{2,1,0:T(2,128)S(1)}, f32[32,2,1024]{2,1,0:T(2,128)}, u32[]{:S(2)}) %copy-start.1) | copy-done | bytes 262168
  2.6 0.0 copy-start.5
  2.6 0.7 copy-done.5
  3.3 1.7 %shard_map.104 = (f32[32,4,1024]{2,1,0:T(4,128)S(1)}, f32[32,4,1024]{2,1,0:T(4,128)S(1)}, f32[16,8,128]{2,1,0:T(8,128)}, s32[1,1024]{1,0:T(1,128)S(1)}) custom-call(f32[32,4,1024]{2,1,0:T(4,128)S(1)} %copy-done, f32[32,2,1024]{2,1,0:T(2,128)S(1)} %copy-done.1, s32[2,1024]{1,0:T(2,128)S(1)} %copy-done.5), custom_call_target="tpu_custom_call" | custom-call | tf_op jit(solution)/shard_map/pallas_call | solution.py:152
  5.0 0.0 copy-start.7
  5.0 0.0 copy-start.8
  5.0 15.9 %all-to-all-start = ((f32[16,8,128]{2,1,0:T(8,128)}), f32[16,8,128]{2,1,0:T(8,128)S(1)}, u32[]{:S(2)}, u32[]{:S(2)}) async-start(f32[16,8,128]{2,1,0:T(8,128)} %get-tuple-element.8), calls=%async_computation | async-start | bytes 131072 | tf_op jit(solution)/shard_map/all_to_all | solution.py:171
  20.9 0.0 copy-done.7
  20.9 0.0 copy-done.8
  20.9 11.5 %all-to-all-done = f32[16,8,128]{2,1,0:T(8,128)S(1)} async-done(((f32[16,8,128]{2,1,0:T(8,128)}), f32[16,8,128]{2,1,0:T(8,128)S(1)}, u32[]{:S(2)}, u32[]{:S(2)}) %all-to-all-start) | async-done | bytes 65568 | tf_op jit(solution)/shard_map/all_to_all | solution.py:171
  32.4 0.7 copy.11
  33.2 0.0 copy-start.6
  33.2 9.3 %all-to-all-start.1 = ((f32[32,4,128]{2,1,0:T(4,128)}), f32[32,4,128]{2,1,0:T(4,128)S(1)}, u32[]{:S(2)}, u32[]{:S(2)}) async-start(f32[32,4,128]{2,1,0:T(4,128)} %bitcast.2), calls=%async_computation.1 | async-start | bytes 131072 | tf_op jit(solution)/shard_map/all_to_all | solution.py:173
  42.5 0.0 copy-start.2
  42.5 0.0 copy-start.3
  42.5 0.0 copy-start.4
  42.6 7.2 %all-to-all-done.1.got_ref = f32[32,4,128]{2,1,0:T(4,128)S(1)} async-done(((f32[32,4,128]{2,1,0:T(4,128)}), f32[32,4,128]{2,1,0:T(4,128)S(1)}, u32[]{:S(2)}, u32[]{:S(2)}) %all-to-all-start.1) | async-done | bytes 65568 | tf_op jit(solution)/shard_map/all_to_all | solution.py:173
  49.8 0.0 copy-done.6
  49.8 0.0 copy-done.2
  49.8 0.0 copy-done.3
  49.8 0.0 copy-done.4
  49.8 1.3 %shard_map.105 = (f32[6,1024]{1,0:T(8,128)}, f32[16,8,128]{2,1,0:T(8,128)S(1)}) custom-call(f32[32,4,128]{2,1,0:T(4,128)S(1)} %all-to-all-done.1.got_ref, f32[6,1024]{1,0:T(8,128)S(1)} %broadcast_divide_fusion.share_ref, f32[6,1024]{1,0:T(8,128)S(1)} %copy-done.2, f32[6,1024]{1,0:T(8,128)S(1)} %copy-done.3, f32[6,1024]{1,0:T(8,128)S(1)} %copy-done.4, ...), custom_call_target="tpu_custom_call" | custom-call | tf_op jit(solution)/shard_map/pallas_call | solution.py:152
  51.1 14.3 %all_to_all.20 = f32[16,8,128]{2,1,0:T(8,128)S(1)} all-to-all(f32[16,8,128]{2,1,0:T(8,128)S(1)} %get-tuple-element.9), channel_id=1, replica_groups=mesh['gx'=16,'gy'=8,'sa'=4] {'gx'}, dimensions={0} | all-to-all | bytes 131072 | tf_op jit(solution)/shard_map/all_to_all | solution.py:171
  65.4 0.1 copy.12
  65.5 12.2 %all_to_all.21.back_ref = f32[32,4,128]{2,1,0:T(4,128)S(1)} all-to-all(f32[32,4,128]{2,1,0:T(4,128)S(1)} %bitcast.10), channel_id=1, replica_groups=mesh['gx'=16,'gy'=8,'sa'=4] {'gy','sa'}, dimensions={0} | all-to-all | bytes 131072 | tf_op jit(solution)/shard_map/all_to_all | solution.py:173
  77.7 1.2 %shard_map.106 = f32[32,4,1024]{2,1,0:T(4,128)} custom-call(f32[32,4,128]{2,1,0:T(4,128)S(1)} %all_to_all.21.back_ref, s32[1,1024]{1,0:T(1,128)S(1)} %get-tuple-element.10.slot_ref, f32[32,4,1024]{2,1,0:T(4,128)S(1)} %get-tuple-element.11.off_ref, f32[32,4,1024]{2,1,0:T(4,128)S(1)} %get-tuple-element.12.fac_ref), custom_call_target="tpu_custom_call" | custom-call | tf_op jit(solution)/shard_map/pallas_call | solution.py:152
  (2 shorter events, 0.0 us)
Async XLA Ops:
  0.6 1.0 %copy-start = (f32[32,4,1024]{2,1,0:T(4,128)S(1)}, f32[32,4,1024]{2,1,0:T(4,128)}, u32[]{:S(2)}) copy-start(f32[32,4,1024]{2,1,0:T(4,128)} %refs_0_.1) | copy-start | bytes 1572868
  1.7 0.9 %copy-start.1 = (f32[32,2,1024]{2,1,0:T(2,128)S(1)}, f32[32,2,1024]{2,1,0:T(2,128)}, u32[]{:S(2)}) copy-start(f32[32,2,1024]{2,1,0:T(2,128)} %refs_1_.1) | copy-start | bytes 786436
  2.6 0.7 copy-start.5
  5.0 15.9 %copy-start.7 = (f32[6,1024]{1,0:T(8,128)S(1)}, f32[6,1024]{1,0:T(8,128)}, u32[]{:S(2)}) copy-start(f32[6,1024]{1,0:T(8,128)} %param.12) | copy-start | bytes 73732
  5.0 15.9 %copy-start.8 = (s32[5,1024]{1,0:T(8,128)S(1)}, s32[5,1024]{1,0:T(8,128)}, u32[]{:S(2)}) copy-start(s32[5,1024]{1,0:T(8,128)} %param.13) | copy-start | bytes 61444
  5.0 27.4 %all-to-all-start = ((f32[16,8,128]{2,1,0:T(8,128)}), f32[16,8,128]{2,1,0:T(8,128)S(1)}, u32[]{:S(2)}, u32[]{:S(2)}) async-start(f32[16,8,128]{2,1,0:T(8,128)} %get-tuple-element.8), calls=%async_computation | async-start | bytes 131072 | tf_op jit(solution)/shard_map/all_to_all | solution.py:171
  33.2 16.6 %copy-start.6 = (f32[2,1024]{1,0:T(2,128)S(1)}, f32[2,1024]{1,0:T(2,128)}, u32[]{:S(2)}) copy-start(f32[2,1024]{1,0:T(2,128)} %drift_ref.1) | copy-start | bytes 24580
  33.2 16.6 %all-to-all-start.1 = ((f32[32,4,128]{2,1,0:T(4,128)}), f32[32,4,128]{2,1,0:T(4,128)S(1)}, u32[]{:S(2)}, u32[]{:S(2)}) async-start(f32[32,4,128]{2,1,0:T(4,128)} %bitcast.2), calls=%async_computation.1 | async-start | bytes 131072 | tf_op jit(solution)/shard_map/all_to_all | solution.py:173
  42.5 7.3 %copy-start.2 = (f32[6,1024]{1,0:T(8,128)S(1)}, f32[6,1024]{1,0:T(8,128)}, u32[]{:S(2)}) copy-start(f32[6,1024]{1,0:T(8,128)} %flux_ref.1) | copy-start | bytes 73732
  42.5 7.3 %copy-start.3 = (f32[6,1024]{1,0:T(8,128)S(1)}, f32[6,1024]{1,0:T(8,128)}, u32[]{:S(2)}) copy-start(f32[6,1024]{1,0:T(8,128)} %link_ref.1) | copy-start | bytes 73732
  42.5 7.3 %copy-start.4 = (f32[6,1024]{1,0:T(8,128)S(1)}, f32[6,1024]{1,0:T(8,128)}, u32[]{:S(2)}) copy-start(f32[6,1024]{1,0:T(8,128)} %bottom_ref.1) | copy-start | bytes 73732

commit v2 on v1

--- a/solution.py
+++ b/solution.py
@@ -9,6 +9,7 @@
 WORDS = 8
 CAP = 4
 LANES = 128
+PIECES = 4
 VAPOUR_ENTHALPY = 2.5
 NT = (((1,), (1,)), ((), ()))
 NN = (((1,), (0,)), ((), ()))
@@ -28,9 +29,51 @@
     return lax.dot_general(a, b, dims, preferred_element_type=jnp.float32)
 
 
-def columns_kernel(far, near, prof_ref, coef_ref, owner_ref, off_ref, fac_ref, send_ref, slot_ref):
+def columns_kernel(
+    far,
+    near,
+    prof_hbm,
+    coef_hbm,
+    owner_hbm,
+    fraction_hbm,
+    flag_hbm,
+    flux_hbm,
+    link_hbm,
+    bottom_hbm,
+    drift_hbm,
+    off_ref,
+    fac_ref,
+    send_ref,
+    slot_ref,
+    share_ref,
+    flux_ref,
+    link_ref,
+    bottom_ref,
+    drift_ref,
+    prof_ref,
+    coef_ref,
+    owner_ref,
+    fraction_ref,
+    flag_ref,
+    sems,
+):
+    pairs = (
+        (owner_hbm, owner_ref),
+        (coef_hbm, coef_ref),
+        (prof_hbm, prof_ref),
+        (fraction_hbm, fraction_ref),
+        (flag_hbm, flag_ref),
+        (flux_hbm, flux_ref),
+        (link_hbm, link_ref),
+        (bottom_hbm, bottom_ref),
+        (drift_hbm, drift_ref),
+    )
+    copies = [pltpu.make_async_copy(a, b, sems.at[k]) for k, (a, b) in enumerate(pairs)]
+    for copy in copies:
+        copy.start()
     levels, fields, n = prof_ref.shape
     scalar_row = lax.broadcasted_iota(jnp.int32, (fields, n), 0) < 2
+    copies[0].wait()
     owner = owner_ref[0:1, :]
     blocks = n // LANES
     tall = jnp.concatenate([owner[:, j * LANES:(j + 1) * LANES] for j in range(blocks)], axis=0).T
@@ -45,7 +88,12 @@
             totals[j] += jnp.sum(same.astype(jnp.int32), axis=0, keepdims=True)
     slot = owner * CAP + jnp.concatenate(totals, axis=1)
     slot_ref[...] = slot
-
+    per_far = near * CAP
+    row = slot // per_far
+    place = one_hot(slot % per_far, per_far)
+
+    copies[1].wait()
+    copies[2].wait()
     above = factor = offset = jnp.zeros((fields, n), jnp.float32)
     for k in range(levels):
         below = jnp.where(scalar_row, coef_ref[k, 0:1, :], coef_ref[k, 1:2, :])
@@ -66,13 +114,20 @@
         ],
         axis=0,
     )
-    per_far = near * CAP
-    row = slot // per_far
     spread = jnp.concatenate([jnp.where(row == g, values, 0.0) for g in range(far)], axis=0)
-    place = one_hot(slot % per_far, per_far)
     sent = dot(jnp.concatenate(halves(spread), axis=0), place, NT)
     rows = far * WORDS
     send_ref[...] = (sent[:rows] + sent[rows:]).reshape(far, WORDS, per_far)
+
+    copies[3].wait()
+    copies[4].wait()
+    water = fraction_ref[0:1, :]
+    ice = fraction_ref[1:, :] * flag_ref[...].astype(jnp.float32)
+    inverse = 1.0 / (water + jnp.sum(ice, axis=0, keepdims=True))
+    share_ref[0:1, :] = water * inverse
+    share_ref[1:, :] = ice * inverse
+    for copy in copies[5:]:
+        copy.wait()
 
 
 def cells_kernel(got_ref, share_ref, flux_ref, link_ref, bottom_ref, drift_ref, kelvin_ref, reply_ref):
@@ -128,9 +183,11 @@
         reply_ref[g] = reply[:, g * per_far:(g + 1) * per_far]
 
 
-def finish_kernel(back_ref, slot_ref, off_ref, fac_ref, out_ref):
+def finish_kernel(back_ref, slot_ref, off_ref, fac_ref, kelvin_ref, out_hbm, kelvin_hbm, out_ref, sems):
     levels, fields, n = off_ref.shape
     near, cap, width = back_ref.shape
+    save_kelvin = pltpu.make_async_copy(kelvin_ref, kelvin_hbm, sems.at[0])
+    save_kelvin.start()
     per_far = near * cap
     far = width // WORDS
     slot = slot_ref[...]
@@ -142,34 +199,38 @@
     for g in range(far):
         level = level + jnp.where(row == g, spread[g * WORDS:(g + 1) * WORDS], 0.0)
     level = level[0:fields]
+    saves = []
+    step = levels // PIECES
     for k in range(levels - 1, -1, -1):
         level = off_ref[k] + fac_ref[k] * level
         out_ref[k] = level
-
-
-def call(kernel, out_shape, *args):
-    vmem = pl.BlockSpec(memory_space=pltpu.VMEM)
+        if k % step == 0:
+            part = pl.ds(k, step)
+            save = pltpu.make_async_copy(out_ref.at[part], out_hbm.at[part], sems.at[1 + k // step])
+            save.start()
+            saves.append(save)
+    for save in saves:
+        save.wait()
+    save_kelvin.wait()
+
+
+def call(kernel, out_shape, in_space, out_spaces, scratch, *args):
+    if in_space == pltpu.HBM:
+        args = [pltpu.with_memory_space_constraint(x, pltpu.HBM) for x in args]
     return pl.pallas_call(
         kernel,
         out_shape=out_shape,
-        in_specs=[vmem] * len(args),
-        out_specs=jax.tree.map(lambda _: vmem, out_shape),
-        compiler_params=pltpu.CompilerParams(vmem_limit_bytes=40 * 1024 * 1024),
+        in_specs=[pl.BlockSpec(memory_space=in_space)] * len(args),
+        out_specs=[pl.BlockSpec(memory_space=space) for space in out_spaces],
+        scratch_shapes=scratch,
+        compiler_params=pltpu.CompilerParams(vmem_limit_bytes=32 * 1024 * 1024),
     )(*args)
 
 
-def surface_weights(kind_fractions, kind_existing_flags):
-    present = jnp.concatenate(
-        [jnp.ones_like(kind_existing_flags[:1]), kind_existing_flags], axis=0
-    ).astype(jnp.float32)
-    unscaled = kind_fractions * present
-    return unscaled / jnp.sum(unscaled, axis=0, keepdims=True)
-
-
 def exchange_parcels(parcels, near):
-    far = parcels.shape[0]
+    far, words, _ = parcels.shape
     parcels = lax.all_to_all(parcels, "gx", split_axis=0, concat_axis=0, tiled=True)
-    parcels = parcels.reshape(far * WORDS, near * CAP).T.reshape(near, CAP, far * WORDS)
+    parcels = parcels.reshape(far * words, near * CAP).T.reshape(near, CAP, far * words)
     return lax.all_to_all(parcels, ("gy", "sa"), split_axis=0, concat_axis=0, tiled=True)
 
 
@@ -177,21 +238,47 @@
     far = lax.axis_size("gx")
     near = lax.axis_size(("gy", "sa"))
     n = profile.shape[2]
-    f32 = jnp.float32
+    f32, i32 = jnp.float32, jnp.int32
     shape = jax.ShapeDtypeStruct
-    share = surface_weights(fractions, flags)
-    parcels = shape((far, WORDS, near * CAP), f32)
-    offsets, factors, send, slot = call(
+    like = lambda x: shape(x.shape, x.dtype)
+    held = lambda x: pltpu.VMEM(x.shape, x.dtype)
+    vmem, hbm = pltpu.VMEM, pltpu.HBM
+    offsets, factors, send, slot, share, flux, links, bottom, drift = call(
         lambda *refs: columns_kernel(far, near, *refs),
-        (shape(profile.shape, f32), shape(profile.shape, f32), parcels, shape((1, n), jnp.int32)),
-        profile, coefficients, owner,
+        [
+            like(profile),
+            like(profile),
+            shape((far, WORDS, near * CAP), f32),
+            shape((1, n), i32),
+            like(fractions),
+            like(flux),
+            like(links),
+            like(bottom),
+            like(drift),
+        ],
+        hbm,
+        [vmem] * 9,
+        [held(x) for x in (profile, coefficients, owner, fractions, flags)] + [pltpu.SemaphoreType.DMA((9,))],
+        profile, coefficients, owner, fractions, flags, flux, links, bottom, drift,
     )
     got = exchange_parcels(send, near)
     kelvin, reply = call(
-        cells_kernel, (shape(bottom.shape, f32), parcels), got, share, flux, links, bottom, drift
+        cells_kernel,
+        [like(bottom), shape((far, WORDS, near * CAP), f32)],
+        vmem,
+        [vmem] * 2,
+        [],
+        got, share, flux, links, bottom, drift,
     )
     back = exchange_parcels(reply, near)
-    advanced = call(finish_kernel, shape(profile.shape, f32), back, slot, offsets, factors)
+    advanced, kelvin = call(
+        finish_kernel,
+        [like(profile), like(bottom)],
+        vmem,
+        [hbm] * 2,
+        [held(profile), pltpu.SemaphoreType.DMA((1 + PIECES,))],
+        back, slot, offsets, factors, kelvin,
+    )
     return advanced, kelvin
 
 

time: 79.3 us -> 75.4 us (0.951)
  blocking collectives: 26.5 us -> 69.9 us
  starting transfers between devices: 25.2 us -> 0 us
  waiting for transfers between devices: 18.7 us -> 0 us
  local copies, waits for them, and re-layouts: 3.53 us -> 0.17 us
    all_to_all x1 -> x2, blocking collectives: 14.3 us -> 41.4 us  [exchange_parcels(): lax.all_to_all(parcels, 'gx', split_axis=0, concat_axis=0, tiled=True)]
    all_to_all x2 -> x0, starting transfers between devices: 25.2 us -> none  [the longest x1 15.9 us: exchange_parcels(): lax.all_to_all(parcels, 'gx', split_axis=0, concat_axis=0, tiled=True)]
    all_to_all x2 -> x0, waiting for transfers between devices: 18.7 us -> none  [the longest x1 11.5 us: exchange_parcels(): lax.all_to_all(parcels, 'gx', split_axis=0, concat_axis=0, tiled=True)]
    all_to_all x1 -> x2, blocking collectives: 12.2 us -> 28.4 us  [exchange_parcels(): lax.all_to_all(parcels, ('gy', 'sa'), split_axis=0, concat_axis=0, tiled=...]
    unnamed x18 -> x0, local copies, waits for them, and re-layouts: 2.71 us -> none
  transfers between devices with their start and end apart: 2 -> 0, of which waited for: 2 -> 0; matrix products, arithmetic and copies ran while one was open for 0% -> 0% of each run, Pallas kernels for 0% -> 0%
where the time goes in v2:
time: 75.4 us; the launch traced here: 75.1 us
  blocking collectives  69.9 us (93%)
  Pallas kernels  4.45 us (6%)
    all_to_all x2, blocking collectives, exchange_parcels(): lax.all_to_all(parcels, 'gx', split_axis=0, concat_axis=0, tiled=True)  41.4 us
    all_to_all x2, blocking collectives, exchange_parcels(): lax.all_to_all(parcels, ('gy', 'sa'), split_axis=0, concat_axis=0, tiled=...  28.4 us
    pallas_call x3, Pallas kernels, call(): pl.pallas_call(kernel, out_shape=out_shape, in_specs=[pl.BlockSpec(memory...  4.45 us

profile of v2, /device:TPU:1, one launch (start us, length us, event | category | flops | bytes accessed | tf_op | source)
XLA Modules:
  0.0 75.1 jit_solution(16628032600079967022)
XLA Ops:
  0.6 2.2 %shard_map.104 = (f32[32,4,1024]{2,1,0:T(4,128)S(1)}, f32[32,4,1024]{2,1,0:T(4,128)S(1)}, f32[16,8,128]{2,1,0:T(8,128)S(1)}, s32[1,1024]{1,0:T(1,128)S(1)}, f32[...) custom-call(f32[32,4,1024]{2,1,0:T(4,128)} %refs_0_.1, ...), custom_call_target="tpu_custom_call" | custom-call | tf_op jit(solution)/shard_map/pallas_call | solution.py:220
  2.9 27.1 %all_to_all.20 = f32[16,8,128]{2,1,0:T(8,128)S(1)} all-to-all(f32[16,8,128]{2,1,0:T(8,128)S(1)} %get-tuple-element.13), channel_id=1, replica_groups=mesh['gx'=16,'gy'=8,'sa'=4] {'gx'}, dimensions={0} | all-to-all | bytes 131072 | tf_op jit(solution)/shard_map/all_to_all | solution.py:232
  30.0 0.1 copy.11
  30.1 16.3 %all_to_all.21.got_ref = f32[32,4,128]{2,1,0:T(4,128)S(1)} all-to-all(f32[32,4,128]{2,1,0:T(4,128)S(1)} %bitcast.9), channel_id=1, replica_groups=mesh['gx'=16,'gy'=8,'sa'=4] {'gy','sa'}, dimensions={0} | all-to-all | bytes 131072 | tf_op jit(solution)/shard_map/all_to_all | solution.py:234
  46.3 1.1 %shard_map.105 = (f32[6,1024]{1,0:T(8,128)S(1)}, f32[16,8,128]{2,1,0:T(8,128)S(1)}) custom-call(f32[32,4,128]{2,1,0:T(4,128)S(1)} %all_to_all.21.got_ref, f32[6,1024]{1,0:T(8,128)S(1)} %get-tuple-element.14.share_ref, f32[6,1024]{1,0:T(8,128)S(1)} %get-tuple-element.15.flux_ref, f32[6,1024]{1,0:T(8,128)S(1)} %get-tuple-element.16.link_ref, ...), custom_call_target="tpu_custom_call" | custom-call | tf_op jit(solution)/shard_map/pallas_call | solution.py:220
  47.4 14.3 %all_to_all.22 = f32[16,8,128]{2,1,0:T(8,128)S(1)} all-to-all(f32[16,8,128]{2,1,0:T(8,128)S(1)} %get-tuple-element.19), channel_id=1, replica_groups=mesh['gx'=16,'gy'=8,'sa'=4] {'gx'}, dimensions={0} | all-to-all | bytes 131072 | tf_op jit(solution)/shard_map/all_to_all | solution.py:232
  61.7 0.1 copy.12
  61.8 12.2 %all_to_all.23.back_ref = f32[32,4,128]{2,1,0:T(4,128)S(1)} all-to-all(f32[32,4,128]{2,1,0:T(4,128)S(1)} %bitcast.11), channel_id=1, replica_groups=mesh['gx'=16,'gy'=8,'sa'=4] {'gy','sa'}, dimensions={0} | all-to-all | bytes 131072 | tf_op jit(solution)/shard_map/all_to_all | solution.py:234
  74.0 1.1 %shard_map.106 = (f32[32,4,1024]{2,1,0:T(4,128)}, f32[6,1024]{1,0:T(8,128)}) custom-call(f32[32,4,128]{2,1,0:T(4,128)S(1)} %all_to_all.23.back_ref, s32[1,1024]{1,0:T(1,128)S(1)} %get-tuple-element.20.slot_ref, f32[32,4,1024]{2,1,0:T(4,128)S(1)} %get-tuple-element.21.off_ref, f32[32,4,1024]{2,1,0:T(4,128)S(1)} %get-tuple-element.22.fac_ref, ...), custom_call_target="tpu_custom_call" | custom-call | tf_op jit(solution)/shard_map/pallas_call | solution.py:220

commit v3 on v2

--- a/solution.py
+++ b/solution.py
@@ -7,9 +7,12 @@
 
 SWEEPS = 3
 WORDS = 8
+SENT = 5
+ANSWERED = 4
 CAP = 4
 LANES = 128
 PIECES = 4
+INP = 1
 VAPOUR_ENTHALPY = 2.5
 NT = (((1,), (1,)), ((), ()))
 NN = (((1,), (0,)), ((), ()))
@@ -57,25 +60,28 @@
     flag_ref,
     sems,
 ):
-    pairs = (
-        (owner_hbm, owner_ref),
-        (coef_hbm, coef_ref),
-        (prof_hbm, prof_ref),
+    levels, rows, _ = prof_ref.shape
+    n = owner_ref.shape[1]
+    blocks = n // LANES
+    fields = rows // blocks
+    step = levels // INP
+    parts = [pl.ds(k * step, step) for k in range(INP)]
+    pairs = [(owner_hbm, owner_ref)]
+    for part in parts:
+        pairs += [(coef_hbm.at[part], coef_ref.at[part]), (prof_hbm.at[part], prof_ref.at[part])]
+    pairs += [
         (fraction_hbm, fraction_ref),
         (flag_hbm, flag_ref),
         (flux_hbm, flux_ref),
         (link_hbm, link_ref),
         (bottom_hbm, bottom_ref),
         (drift_hbm, drift_ref),
-    )
+    ]
     copies = [pltpu.make_async_copy(a, b, sems.at[k]) for k, (a, b) in enumerate(pairs)]
     for copy in copies:
         copy.start()
-    levels, fields, n = prof_ref.shape
-    scalar_row = lax.broadcasted_iota(jnp.int32, (fields, n), 0) < 2
     copies[0].wait()
     owner = owner_ref[0:1, :]
-    blocks = n // LANES
     tall = jnp.concatenate([owner[:, j * LANES:(j + 1) * LANES] for j in range(blocks)], axis=0).T
     earlier = lax.broadcasted_iota(jnp.int32, (LANES, LANES), 0) < lax.broadcasted_iota(jnp.int32, (LANES, LANES), 1)
     totals = [jnp.zeros((1, LANES), jnp.int32) for _ in range(blocks)]
@@ -92,41 +98,65 @@
     row = slot // per_far
     place = one_hot(slot % per_far, per_far)
 
-    copies[1].wait()
-    copies[2].wait()
-    above = factor = offset = jnp.zeros((fields, n), jnp.float32)
+    pair = lax.broadcasted_iota(jnp.int32, (8, LANES), 0) // 2
+    above = last = before = shift = None
     for k in range(levels):
-        below = jnp.where(scalar_row, coef_ref[k, 0:1, :], coef_ref[k, 1:2, :])
-        inverse = 1.0 / (1.0 + above * (1.0 - factor) + below)
-        offset = (prof_ref[k] + above * offset) * inverse
-        factor = below * inverse
-        above = below
+        if k % step == 0:
+            copies[1 + 2 * (k // step)].wait()
+            copies[2 + 2 * (k // step)].wait()
+        below = jnp.concatenate(
+            [
+                jnp.take_along_axis(
+                    coef_ref[k, 8 * (j // 2):8 * (j // 2) + 8], pair + 4 * (j % 2), axis=0, mode="promise_in_bounds"
+                )
+                for j in range(rows // 8)
+            ],
+            axis=0,
+        )
+        if k == 0:
+            now, shift, numerator = 1.0 + below, prof_ref[k], below
+        else:
+            now = (1.0 + above + below) * last
+            if k > 1:
+                now = now - above * above * before
+            else:
+                now = now - above * above
+            shift = prof_ref[k] * last + above * shift
+            numerator = below * last
+        inverse = 1.0 / now
+        offset = shift * inverse
+        factor = numerator * inverse
         off_ref[k] = offset
         fac_ref[k] = factor
-
-    values = jnp.concatenate(
-        [
-            (owner_ref[1:2, :] + 1).astype(jnp.float32),
-            offset[0:2],
-            factor[0:1],
-            above[0:1],
-            jnp.zeros((WORDS - 5, n), jnp.float32),
-        ],
-        axis=0,
-    )
+        above, before, last = below, last, now
+
+    values = []
+    for t in range(blocks):
+        at = fields * t
+        code = (owner_ref[1:2, t * LANES:(t + 1) * LANES] + 1).astype(jnp.float32)
+        values.append(
+            jnp.concatenate(
+                [offset[at:at + 2], factor[at:at + 1], below[at:at + 1], code, jnp.zeros((WORDS - 5, LANES), jnp.float32)],
+                axis=0,
+            )
+        )
+    values = jnp.concatenate(values, axis=1)
     spread = jnp.concatenate([jnp.where(row == g, values, 0.0) for g in range(far)], axis=0)
     sent = dot(jnp.concatenate(halves(spread), axis=0), place, NT)
-    rows = far * WORDS
-    send_ref[...] = (sent[:rows] + sent[rows:]).reshape(far, WORDS, per_far)
-
-    copies[3].wait()
-    copies[4].wait()
+    half = far * WORDS
+    sent = sent[:half] + sent[half:]
+    for g in range(far):
+        send_ref[g] = sent[g * WORDS:g * WORDS + SENT]
+
+    rest = copies[1 + 2 * INP:]
+    rest[0].wait()
+    rest[1].wait()
     water = fraction_ref[0:1, :]
     ice = fraction_ref[1:, :] * flag_ref[...].astype(jnp.float32)
     inverse = 1.0 / (water + jnp.sum(ice, axis=0, keepdims=True))
     share_ref[0:1, :] = water * inverse
     share_ref[1:, :] = ice * inverse
-    for copy in copies[5:]:
+    for copy in rest[2:]:
         copy.wait()
 
 
@@ -137,7 +167,7 @@
     blocks = n // LANES
     got = got_ref[...].reshape(per_far, far * WORDS).T
     got = jnp.concatenate([got[g * WORDS:(g + 1) * WORDS] for g in range(far)], axis=1)
-    cell = got[0:1].astype(jnp.int32) - 1
+    cell = got[4:5].astype(jnp.int32) - 1
     block = cell // LANES
     block = jnp.where(cell < 0, -1, block)
     place = one_hot(cell % LANES, LANES)
@@ -146,7 +176,7 @@
     held = dot(jnp.concatenate(halves(spread), axis=0), place, NT)
     held = held[:rows] + held[rows:]
     held = jnp.concatenate([held[b * WORDS:(b + 1) * WORDS] for b in range(blocks)], axis=1)
-    heat_offset, moist_offset, factor, exchange = (held[k:k + 1] for k in range(1, 5))
+    heat_offset, moist_offset, factor, exchange = (held[k:k + 1] for k in range(4))
 
     share, flux, link, bottom = share_ref[...], flux_ref[...], link_ref[...], bottom_ref[...]
     temp = bottom
@@ -180,11 +210,14 @@
     for b in range(blocks):
         reply = reply + jnp.where(block == b, spread[b * WORDS:(b + 1) * WORDS], 0.0)
     for g in range(far):
-        reply_ref[g] = reply[:, g * per_far:(g + 1) * per_far]
+        reply_ref[g] = reply[0:ANSWERED, g * per_far:(g + 1) * per_far]
 
 
 def finish_kernel(back_ref, slot_ref, off_ref, fac_ref, kelvin_ref, out_hbm, kelvin_hbm, out_ref, sems):
-    levels, fields, n = off_ref.shape
+    levels, rows, _ = off_ref.shape
+    n = slot_ref.shape[1]
+    blocks = n // LANES
+    fields = rows // blocks
     near, cap, width = back_ref.shape
     save_kelvin = pltpu.make_async_copy(kelvin_ref, kelvin_hbm, sems.at[0])
     save_kelvin.start()
@@ -198,7 +231,7 @@
     level = jnp.zeros((WORDS, n), jnp.float32)
     for g in range(far):
         level = level + jnp.where(row == g, spread[g * WORDS:(g + 1) * WORDS], 0.0)
-    level = level[0:fields]
+    level = jnp.concatenate([level[0:fields, t * LANES:(t + 1) * LANES] for t in range(blocks)], axis=0)
     saves = []
     step = levels // PIECES
     for k in range(levels - 1, -1, -1):
@@ -230,14 +263,28 @@
 def exchange_parcels(parcels, near):
     far, words, _ = parcels.shape
     parcels = lax.all_to_all(parcels, "gx", split_axis=0, concat_axis=0, tiled=True)
-    parcels = parcels.reshape(far * words, near * CAP).T.reshape(near, CAP, far * words)
+    parcels = jnp.pad(parcels, ((0, 0), (0, WORDS - words), (0, 0)))
+    parcels = parcels.reshape(far * WORDS, near * CAP).T.reshape(near, CAP, far * WORDS)
     return lax.all_to_all(parcels, ("gy", "sa"), split_axis=0, concat_axis=0, tiled=True)
+
+
+def blocked(x):
+    levels, fields, n = x.shape
+    x = x.reshape(levels, fields, n // LANES, LANES).transpose(0, 2, 1, 3)
+    return x.reshape(levels, fields * n // LANES, LANES)
+
+
+def unblocked(x, fields):
+    levels, rows, _ = x.shape
+    x = x.reshape(levels, rows // fields, fields, LANES).transpose(0, 2, 1, 3)
+    return x.reshape(levels, fields, rows * LANES // fields)
 
 
 def per_device(profile, coefficients, owner, fractions, flags, flux, links, bottom, drift):
     far = lax.axis_size("gx")
     near = lax.axis_size(("gy", "sa"))
-    n = profile.shape[2]
+    fields, n = profile.shape[1:]
+    profile, coefficients = blocked(profile), blocked(coefficients)
     f32, i32 = jnp.float32, jnp.int32
     shape = jax.ShapeDtypeStruct
     like = lambda x: shape(x.shape, x.dtype)
@@ -248,7 +295,7 @@
         [
             like(profile),
             like(profile),
-            shape((far, WORDS, near * CAP), f32),
+            shape((far, SENT, near * CAP), f32),
             shape((1, n), i32),
             like(fractions),
             like(flux),
@@ -258,13 +305,13 @@
         ],
         hbm,
         [vmem] * 9,
-        [held(x) for x in (profile, coefficients, owner, fractions, flags)] + [pltpu.SemaphoreType.DMA((9,))],
+        [held(x) for x in (profile, coefficients, owner, fractions, flags)] + [pltpu.SemaphoreType.DMA((7 + 2 * INP,))],
         profile, coefficients, owner, fractions, flags, flux, links, bottom, drift,
     )
     got = exchange_parcels(send, near)
     kelvin, reply = call(
         cells_kernel,
-        [like(bottom), shape((far, WORDS, near * CAP), f32)],
+        [like(bottom), shape((far, ANSWERED, near * CAP), f32)],
         vmem,
         [vmem] * 2,
         [],
@@ -279,7 +326,7 @@
         [held(profile), pltpu.SemaphoreType.DMA((1 + PIECES,))],
         back, slot, offsets, factors, kelvin,
     )
-    return advanced, kelvin
+    return unblocked(advanced, fields), kelvin
 
 
 def solution(mesh):

time: 75.4 us -> 75 us (level)
  no operation moved by 1% of the time
where the time goes in v3:
time: 75 us; the launch traced here: 74.7 us
  blocking collectives  69.7 us (93%)
  Pallas kernels  4.1 us (5%)
    all_to_all x2, blocking collectives, exchange_parcels(): lax.all_to_all(parcels, 'gx', split_axis=0, concat_axis=0, tiled=True)  41.1 us
    all_to_all x2, blocking collectives, exchange_parcels(): lax.all_to_all(parcels, ('gy', 'sa'), split_axis=0, concat_axis=0, tiled=...  28.6 us
    pallas_call x3, Pallas kernels, call(): pl.pallas_call(kernel, out_shape=out_shape, in_specs=[pl.BlockSpec(memory...  4.1 us

profile of v3, /device:TPU:1, one launch (start us, length us, event | category | flops | bytes accessed | tf_op | source)
XLA Modules:
  0.0 74.7 jit_solution(8741666208463555877)
XLA Ops:
  0.6 1.9 %shard_map.104 = (f32[32,32,128]{2,1,0:T(8,128)S(1)}, f32[32,32,128]{2,1,0:T(8,128)S(1)}, f32[16,5,128]{2,1,0:T(8,128)S(1)}, s32[1,1024]{1,0:T(1,128)S(1)}, f32[...) custom-call(f32[32,32,128]{2,1,0:T(8,128)} %bitcast.25, ...), custom_call_target="tpu_custom_call" | custom-call | tf_op jit(solution)/shard_map/pallas_call | solution.py:253
  2.5 27.1 %all_to_all.20 = f32[16,5,128]{2,1,0:T(8,128)S(1)} all-to-all(f32[16,5,128]{2,1,0:T(8,128)S(1)} %get-tuple-element.15), channel_id=1, replica_groups=mesh['gx'=16,'gy'=8,'sa'=4] {'gx'}, dimensions={0} | all-to-all | bytes 81920 | tf_op jit(solution)/shard_map/all_to_all | solution.py:265
  29.6 0.1 copy.13
  29.7 16.3 %all_to_all.21.got_ref = f32[32,4,128]{2,1,0:T(4,128)S(1)} all-to-all(f32[32,4,128]{2,1,0:T(4,128)S(1)} %bitcast.26), channel_id=1, replica_groups=mesh['gx'=16,'gy'=8,'sa'=4] {'gy','sa'}, dimensions={0} | all-to-all | bytes 131072 | tf_op jit(solution)/shard_map/all_to_all | solution.py:268
  46.0 1.1 %shard_map.105 = (f32[6,1024]{1,0:T(8,128)S(1)}, f32[16,4,128]{2,1,0:T(4,128)S(1)}) custom-call(f32[32,4,128]{2,1,0:T(4,128)S(1)} %all_to_all.21.got_ref, f32[6,1024]{1,0:T(8,128)S(1)} %get-tuple-element.16.share_ref, f32[6,1024]{1,0:T(8,128)S(1)} %get-tuple-element.17.flux_ref, f32[6,1024]{1,0:T(8,128)S(1)} %get-tuple-element.18.link_ref, ...), custom_call_target="tpu_custom_call" | custom-call | tf_op jit(solution)/shard_map/pallas_call | solution.py:253
  47.1 14.0 %all_to_all.22 = f32[16,4,128]{2,1,0:T(4,128)S(1)} all-to-all(f32[16,4,128]{2,1,0:T(4,128)S(1)} %get-tuple-element.21), channel_id=1, replica_groups=mesh['gx'=16,'gy'=8,'sa'=4] {'gx'}, dimensions={0} | all-to-all | bytes 65536 | tf_op jit(solution)/shard_map/all_to_all | solution.py:265
  61.1 0.1 copy.14
  61.2 12.3 %all_to_all.23.back_ref = f32[32,4,128]{2,1,0:T(4,128)S(1)} all-to-all(f32[32,4,128]{2,1,0:T(4,128)S(1)} %bitcast.27), channel_id=1, replica_groups=mesh['gx'=16,'gy'=8,'sa'=4] {'gy','sa'}, dimensions={0} | all-to-all | bytes 131072 | tf_op jit(solution)/shard_map/all_to_all | solution.py:268
  73.5 1.1 %shard_map.106 = (f32[32,32,128]{2,1,0:T(8,128)}, f32[6,1024]{1,0:T(8,128)}) custom-call(f32[32,4,128]{2,1,0:T(4,128)S(1)} %all_to_all.23.back_ref, s32[1,1024]{1,0:T(1,128)S(1)} %get-tuple-element.22.slot_ref, f32[32,32,128]{2,1,0:T(8,128)S(1)} %get-tuple-element.23.off_ref, f32[32,32,128]{2,1,0:T(8,128)S(1)} %get-tuple-element.24.fac_ref, ...), custom_call_target="tpu_custom_call" | custom-call | tf_op jit(solution)/shard_map/pallas_call | solution.py:253
  (2 shorter events, 0.0 us)

commit v4 on v3

--- a/solution.py
+++ b/solution.py
@@ -6,6 +6,8 @@
 from jax.sharding import PartitionSpec as P
 
 SWEEPS = 3
+FAR_FIRST = (8, 8)
+NEAR_FIRST = (22, 22)
 WORDS = 8
 SENT = 5
 ANSWERED = 4
@@ -92,11 +94,12 @@
             if i == j:
                 same = same & earlier
             totals[j] += jnp.sum(same.astype(jnp.int32), axis=0, keepdims=True)
-    slot = owner * CAP + jnp.concatenate(totals, axis=1)
-    slot_ref[...] = slot
     per_far = near * CAP
-    row = slot // per_far
-    place = one_hot(slot % per_far, per_far)
+    row = (owner // near + (far - FAR_FIRST[0])) % far
+    lane = (owner % near + (near - NEAR_FIRST[0])) % near * CAP + jnp.concatenate(totals, axis=1)
+    slot_ref[0:1] = row
+    slot_ref[1:2] = lane
+    place = one_hot(lane, per_far)
 
     pair = lax.broadcasted_iota(jnp.int32, (8, LANES), 0) // 2
     above = last = before = shift = None
@@ -206,11 +209,15 @@
     )
     answer = jnp.concatenate([answer[:, b * LANES:(b + 1) * LANES] for b in range(blocks)], axis=0)
     spread = dot(jnp.concatenate(halves(answer), axis=1), jnp.concatenate([place, place], axis=0), NN)
+    shift = (NEAR_FIRST[0] - NEAR_FIRST[1]) * CAP % per_far
     reply = jnp.zeros((WORDS, far * per_far), jnp.float32)
     for b in range(blocks):
         reply = reply + jnp.where(block == b, spread[b * WORDS:(b + 1) * WORDS], 0.0)
     for g in range(far):
-        reply_ref[g] = reply[0:ANSWERED, g * per_far:(g + 1) * per_far]
+        part = reply[0:ANSWERED, g * per_far:(g + 1) * per_far]
+        if shift:
+            part = jnp.concatenate([part[:, per_far - shift:], part[:, :per_far - shift]], axis=1)
+        reply_ref[(g + FAR_FIRST[0] - FAR_FIRST[1]) % far] = part
 
 
 def finish_kernel(back_ref, slot_ref, off_ref, fac_ref, kelvin_ref, out_hbm, kelvin_hbm, out_ref, sems):
@@ -223,9 +230,9 @@
     save_kelvin.start()
     per_far = near * cap
     far = width // WORDS
-    slot = slot_ref[...]
-    row = slot // per_far
-    place = one_hot(slot % per_far, per_far)
+    row = (slot_ref[0:1] + (far + FAR_FIRST[0] - FAR_FIRST[1])) % far
+    shift = (NEAR_FIRST[0] - NEAR_FIRST[1]) * CAP % per_far
+    place = one_hot((slot_ref[1:2] + shift) % per_far, per_far)
     back = back_ref[...].reshape(per_far, width).T
     spread = dot(jnp.concatenate(halves(back), axis=1), jnp.concatenate([place, place], axis=0), NN)
     level = jnp.zeros((WORDS, n), jnp.float32)
@@ -260,12 +267,17 @@
     )(*args)
 
 
-def exchange_parcels(parcels, near):
+def exchange_parcels(parcels, near, far_first, near_first):
     far, words, _ = parcels.shape
-    parcels = lax.all_to_all(parcels, "gx", split_axis=0, concat_axis=0, tiled=True)
+    axes = ("gx", "gy", "sa")
+    far_order = [(k + far_first) % far for k in range(far)]
+    near_order = [(k + near_first) % near for k in range(near)]
+    far_groups = [[f * near + q for f in far_order] for q in range(near)]
+    near_groups = [[f * near + q for q in near_order] for f in range(far)]
+    parcels = lax.all_to_all(parcels, axes, 0, 0, axis_index_groups=far_groups, tiled=True)
     parcels = jnp.pad(parcels, ((0, 0), (0, WORDS - words), (0, 0)))
     parcels = parcels.reshape(far * WORDS, near * CAP).T.reshape(near, CAP, far * WORDS)
-    return lax.all_to_all(parcels, ("gy", "sa"), split_axis=0, concat_axis=0, tiled=True)
+    return lax.all_to_all(parcels, axes, 0, 0, axis_index_groups=near_groups, tiled=True)
 
 
 def blocked(x):
@@ -296,7 +308,7 @@
             like(profile),
             like(profile),
             shape((far, SENT, near * CAP), f32),
-            shape((1, n), i32),
+            shape((2, n), i32),
             like(fractions),
             like(flux),
             like(links),
@@ -308,7 +320,7 @@
         [held(x) for x in (profile, coefficients, owner, fractions, flags)] + [pltpu.SemaphoreType.DMA((7 + 2 * INP,))],
         profile, coefficients, owner, fractions, flags, flux, links, bottom, drift,
     )
-    got = exchange_parcels(send, near)
+    got = exchange_parcels(send, near, FAR_FIRST[0], NEAR_FIRST[0])
     kelvin, reply = call(
         cells_kernel,
         [like(bottom), shape((far, ANSWERED, near * CAP), f32)],
@@ -317,7 +329,7 @@
         [],
         got, share, flux, links, bottom, drift,
     )
-    back = exchange_parcels(reply, near)
+    back = exchange_parcels(reply, near, FAR_FIRST[1], NEAR_FIRST[1])
     advanced, kelvin = call(
         finish_kernel,
         [like(profile), like(bottom)],

time: 75 us -> 64.9 us (0.87)
  blocking collectives: 69.7 us -> 59.6 us
    all_to_all x4, blocking collectives: 69.7 us -> 59.6 us  [the longest x2 35.9 us: exchange_parcels(): lax.all_to_all(parcels, axes, 0, 0, axis_index_groups=far_groups, tiled=T...]
where the time goes in v4:
time: 64.9 us; the launch traced here: 64.6 us
  blocking collectives  59.6 us (92%)
  Pallas kernels  4.09 us (6%)
  between operations  0.67 us (1%)
    all_to_all x2, blocking collectives, exchange_parcels(): lax.all_to_all(parcels, axes, 0, 0, axis_index_groups=far_groups, tiled=T...  35.9 us
    all_to_all x2, blocking collectives, exchange_parcels(): lax.all_to_all(parcels, axes, 0, 0, axis_index_groups=near_groups, tiled=...  23.7 us
    pallas_call x3, Pallas kernels, call(): pl.pallas_call(kernel, out_shape=out_shape, in_specs=[pl.BlockSpec(memory...  4.09 us

profile of v4, /device:TPU:1, one launch (start us, length us, event | category | flops | bytes accessed | tf_op | source)
XLA Modules:
  0.0 64.6 jit_solution(12483168040196124172)
XLA Ops:
  0.6 1.9 %shard_map.104 = (f32[32,32,128]{2,1,0:T(8,128)S(1)}, f32[32,32,128]{2,1,0:T(8,128)S(1)}, f32[16,5,128]{2,1,0:T(8,128)S(1)}, s32[2,1024]{1,0:T(2,128)S(1)}, f32[...) custom-call(f32[32,32,128]{2,1,0:T(8,128)} %bitcast.25, ...), custom_call_target="tpu_custom_call" | custom-call | tf_op jit(solution)/shard_map/pallas_call | solution.py:260
  2.5 22.2 %all_to_all.20 = f32[16,5,128]{2,1,0:T(8,128)S(1)} all-to-all(f32[16,5,128]{2,1,0:T(8,128)S(1)} %get-tuple-element.15), channel_id=1, replica_groups={{256,288,320,352,384,416,448,480,0,32,64,96,128,160,192,224},{257,289,3..., dimensions={0} | all-to-all | bytes 81920 | tf_op jit(solution)/shard_map/all_to_all | solution.py:277
  24.7 0.1 copy.13
  24.8 12.2 %all_to_all.21.got_ref = f32[32,4,128]{2,1,0:T(4,128)S(1)} all-to-all(f32[32,4,128]{2,1,0:T(4,128)S(1)} %bitcast.26), channel_id=1, replica_groups={{22,23,24,25,26,27,28,29,30,31,0,1,2,3,4,5,6,7,8,9,10,11,12,13,14,15,16..., dimensions={0} | all-to-all | bytes 131072 | tf_op jit(solution)/shard_map/all_to_all | solution.py:280
  37.0 1.1 %shard_map.105 = (f32[6,1024]{1,0:T(8,128)S(1)}, f32[16,4,128]{2,1,0:T(4,128)S(1)}) custom-call(f32[32,4,128]{2,1,0:T(4,128)S(1)} %all_to_all.21.got_ref, f32[6,1024]{1,0:T(8,128)S(1)} %get-tuple-element.16.share_ref, f32[6,1024]{1,0:T(8,128)S(1)} %get-tuple-element.17.flux_ref, f32[6,1024]{1,0:T(8,128)S(1)} %get-tuple-element.18.link_ref, ...), custom_call_target="tpu_custom_call" | custom-call | tf_op jit(solution)/shard_map/pallas_call | solution.py:260
  38.1 13.7 %all_to_all.22 = f32[16,4,128]{2,1,0:T(4,128)S(1)} all-to-all(f32[16,4,128]{2,1,0:T(4,128)S(1)} %get-tuple-element.21), channel_id=1, replica_groups={{256,288,320,352,384,416,448,480,0,32,64,96,128,160,192,224},{257,289,3..., dimensions={0} | all-to-all | bytes 65536 | tf_op jit(solution)/shard_map/all_to_all | solution.py:277
  51.8 0.1 copy.14
  51.9 11.5 %all_to_all.23.back_ref = f32[32,4,128]{2,1,0:T(4,128)S(1)} all-to-all(f32[32,4,128]{2,1,0:T(4,128)S(1)} %bitcast.27), channel_id=1, replica_groups={{22,23,24,25,26,27,28,29,30,31,0,1,2,3,4,5,6,7,8,9,10,11,12,13,14,15,16..., dimensions={0} | all-to-all | bytes 131072 | tf_op jit(solution)/shard_map/all_to_all | solution.py:280
  63.4 1.1 %shard_map.106 = (f32[32,32,128]{2,1,0:T(8,128)}, f32[6,1024]{1,0:T(8,128)}) custom-call(f32[32,4,128]{2,1,0:T(4,128)S(1)} %all_to_all.23.back_ref, s32[2,1024]{1,0:T(2,128)S(1)} %get-tuple-element.22.slot_ref, f32[32,32,128]{2,1,0:T(8,128)S(1)} %get-tuple-element.23.off_ref, f32[32,32,128]{2,1,0:T(8,128)S(1)} %get-tuple-element.24.fac_ref, ...), custom_call_target="tpu_custom_call" | custom-call | tf_op jit(solution)/shard_map/pallas_call | solution.py:260
  (2 shorter events, 0.0 us)

commit v5 on v4

--- a/solution.py
+++ b/solution.py
@@ -23,6 +23,11 @@
 def halves(x):
     high = x.astype(jnp.bfloat16)
     return high, (x - high.astype(jnp.float32)).astype(jnp.bfloat16)
+
+
+def stacked_halves(x):
+    high = x.astype(jnp.bfloat16).astype(jnp.float32)
+    return jnp.concatenate([high, x - high], axis=0)
 
 
 def one_hot(index_row, count):
@@ -51,7 +56,7 @@
     send_ref,
     slot_ref,
     share_ref,
-    flux_ref,
+    base_ref,
     link_ref,
     bottom_ref,
     drift_ref,
@@ -60,6 +65,10 @@
     owner_ref,
     fraction_ref,
     flag_ref,
+    flux_in,
+    link_in,
+    bottom_in,
+    drift_in,
     sems,
 ):
     levels, rows, _ = prof_ref.shape
@@ -74,10 +83,10 @@
     pairs += [
         (fraction_hbm, fraction_ref),
         (flag_hbm, flag_ref),
-        (flux_hbm, flux_ref),
-        (link_hbm, link_ref),
-        (bottom_hbm, bottom_ref),
-        (drift_hbm, drift_ref),
+        (flux_hbm, flux_in),
+        (link_hbm, link_in),
+        (bottom_hbm, bottom_in),
+        (drift_hbm, drift_in),
     ]
     copies = [pltpu.make_async_copy(a, b, sems.at[k]) for k, (a, b) in enumerate(pairs)]
     for copy in copies:
@@ -143,90 +152,105 @@
                 axis=0,
             )
         )
-    values = jnp.concatenate(values, axis=1)
-    spread = jnp.concatenate([jnp.where(row == g, values, 0.0) for g in range(far)], axis=0)
-    sent = dot(jnp.concatenate(halves(spread), axis=0), place, NT)
-    half = far * WORDS
-    sent = sent[:half] + sent[half:]
+    values = stacked_halves(jnp.concatenate(values, axis=1))
+    spread = jnp.concatenate([jnp.where(row == g, values, 0.0).astype(jnp.bfloat16) for g in range(far)], axis=0)
+    sent = dot(spread, place, NT)
     for g in range(far):
-        send_ref[g] = sent[g * WORDS:g * WORDS + SENT]
+        at = 2 * g * WORDS
+        send_ref[g] = sent[at:at + SENT] + sent[at + WORDS:at + WORDS + SENT]
 
     rest = copies[1 + 2 * INP:]
     rest[0].wait()
     rest[1].wait()
-    water = fraction_ref[0:1, :]
-    ice = fraction_ref[1:, :] * flag_ref[...].astype(jnp.float32)
-    inverse = 1.0 / (water + jnp.sum(ice, axis=0, keepdims=True))
-    share_ref[0:1, :] = water * inverse
-    share_ref[1:, :] = ice * inverse
+    present = flag_ref[...].astype(jnp.float32)
+    for t in range(blocks):
+        part = slice(t * LANES, (t + 1) * LANES)
+        share_ref[0:1, t] = fraction_ref[0:1, part]
+        share_ref[1:, t] = fraction_ref[1:, part] * present[:, part]
+    inverse = 1.0 / jnp.sum(share_ref[...], axis=0)
+    for kind in range(share_ref.shape[0]):
+        share_ref[kind] = share_ref[kind] * inverse
     for copy in rest[2:]:
         copy.wait()
-
-
-def cells_kernel(got_ref, share_ref, flux_ref, link_ref, bottom_ref, drift_ref, kelvin_ref, reply_ref):
+    for t in range(blocks):
+        part = slice(t * LANES, (t + 1) * LANES)
+        link, bottom = link_in[:, part], bottom_in[:, part]
+        base_ref[:, t] = flux_in[:, part] + link * bottom
+        link_ref[:, t] = link
+        bottom_ref[:, t] = bottom
+        drift_ref[:, t] = drift_in[:, part]
+
+
+def cells_kernel(got_ref, share_ref, base_ref, link_ref, bottom_ref, drift_ref, kelvin_ref, reply_ref, answer_ref):
     far = reply_ref.shape[0]
     per_far = reply_ref.shape[2]
-    n = share_ref.shape[1]
-    blocks = n // LANES
+    kinds, blocks, _ = share_ref.shape
     got = got_ref[...].reshape(per_far, far * WORDS).T
-    got = jnp.concatenate([got[g * WORDS:(g + 1) * WORDS] for g in range(far)], axis=1)
-    cell = got[4:5].astype(jnp.int32) - 1
-    block = cell // LANES
-    block = jnp.where(cell < 0, -1, block)
+    high = got.astype(jnp.bfloat16).astype(jnp.float32)
+    low = got - high
+    word = lambda x, w: jnp.concatenate([x[g * WORDS + w:g * WORDS + w + 1] for g in range(far)], axis=1)
+    cell = word(got, 4).astype(jnp.int32) - 1
+    block = jnp.where(cell < 0, -1, cell // LANES)
     place = one_hot(cell % LANES, LANES)
-    spread = jnp.concatenate([jnp.where(block == b, got, 0.0) for b in range(blocks)], axis=0)
-    rows = blocks * WORDS
-    held = dot(jnp.concatenate(halves(spread), axis=0), place, NT)
-    held = held[:rows] + held[rows:]
-    held = jnp.concatenate([held[b * WORDS:(b + 1) * WORDS] for b in range(blocks)], axis=1)
-    heat_offset, moist_offset, factor, exchange = (held[k:k + 1] for k in range(4))
-
-    share, flux, link, bottom = share_ref[...], flux_ref[...], link_ref[...], bottom_ref[...]
+    own = lax.broadcasted_iota(jnp.int32, (blocks, far * per_far), 0) == block
+    spread = [jnp.where(own, word(x, w), 0.0) for w in range(4) for x in (high, low)]
+    held = dot(jnp.concatenate(spread, axis=0).astype(jnp.bfloat16), place, NT)
+    heat_offset, moist_offset, factor, exchange = (
+        held[2 * w * blocks:(2 * w + 1) * blocks] + held[(2 * w + 1) * blocks:(2 * w + 2) * blocks] for w in range(4)
+    )
+
+    share = [share_ref[k] for k in range(kinds)]
+    bottom = [bottom_ref[k] for k in range(kinds)]
+    moist_pull = VAPOUR_ENTHALPY * exchange
+    column_part = exchange * heat_offset + moist_pull * moist_offset
+    heat_mix, moist_mix = exchange * factor, moist_pull * factor
+    base = [base_ref[k] + column_part for k in range(kinds)]
+    pull = [link_ref[k] + exchange for k in range(kinds)]
     temp = bottom
     for _ in range(SWEEPS):
-        sat = 0.6 * jnp.exp(0.3 * temp)
-        air_heat = heat_offset + factor * jnp.sum(share * temp, axis=0, keepdims=True)
-        air_moist = moist_offset + factor * jnp.sum(share * sat, axis=0, keepdims=True)
-        emitted = 0.5 * jnp.exp(0.2 * temp)
-        residual = (
-            flux
-            - emitted
-            - exchange * (temp - air_heat)
-            - VAPOUR_ENTHALPY * exchange * (sat - air_moist)
-            - link * (temp - bottom)
-        )
-        slope = 0.2 * emitted + exchange * (1.0 + VAPOUR_ENTHALPY * 0.3 * sat) + link
-        temp = temp + residual / slope
-    kelvin_ref[...] = temp
-    answer = jnp.concatenate(
-        [
-            jnp.sum(share * temp, axis=0, keepdims=True),
-            jnp.sum(share * (0.6 * jnp.exp(0.3 * temp)), axis=0, keepdims=True),
-            drift_ref[...],
-            jnp.zeros((WORDS - 4, n), jnp.float32),
-        ],
-        axis=0,
-    )
-    answer = jnp.concatenate([answer[:, b * LANES:(b + 1) * LANES] for b in range(blocks)], axis=0)
-    spread = dot(jnp.concatenate(halves(answer), axis=1), jnp.concatenate([place, place], axis=0), NN)
+        sat = [0.6 * jnp.exp(0.3 * t) for t in temp]
+        emitted = [0.5 * jnp.exp(0.2 * t) for t in temp]
+        mixed = heat_mix * sum(a * t for a, t in zip(share, temp)) + moist_mix * sum(a * q for a, q in zip(share, sat))
+        for k in range(kinds):
+            residual = (base[k] + mixed) - emitted[k] - pull[k] * temp[k] - moist_pull * sat[k]
+            slope = 0.2 * emitted[k] + (0.3 * moist_pull) * sat[k] + pull[k]
+            temp = temp[:k] + [temp[k] + residual / slope] + temp[k + 1:]
+    for k in range(kinds):
+        kelvin_ref[k] = temp[k]
+    answers = (
+        sum(a * t for a, t in zip(share, temp)),
+        sum(a * (0.6 * jnp.exp(0.3 * t)) for a, t in zip(share, temp)),
+        drift_ref[0],
+        drift_ref[1],
+    )
+    for w, answer in enumerate(answers):
+        answer_ref[pl.ds(w, blocks, stride=ANSWERED)] = answer
+    spread = dot(
+        jnp.concatenate(halves(answer_ref[...]), axis=1), jnp.concatenate([place, place], axis=0), NN
+    )
+    two = 2 * ANSWERED
+    first = lax.broadcasted_iota(jnp.int32, (two, far * per_far), 0) // ANSWERED
+    reply = jnp.zeros((two, far * per_far), jnp.float32)
+    for b in range(0, blocks, 2):
+        reply = reply + jnp.where(first == block - b, spread[b * ANSWERED:b * ANSWERED + two], 0.0)
+    reply = reply[:ANSWERED] + reply[ANSWERED:]
     shift = (NEAR_FIRST[0] - NEAR_FIRST[1]) * CAP % per_far
-    reply = jnp.zeros((WORDS, far * per_far), jnp.float32)
-    for b in range(blocks):
-        reply = reply + jnp.where(block == b, spread[b * WORDS:(b + 1) * WORDS], 0.0)
     for g in range(far):
-        part = reply[0:ANSWERED, g * per_far:(g + 1) * per_far]
+        part = reply[:, g * per_far:(g + 1) * per_far]
         if shift:
             part = jnp.concatenate([part[:, per_far - shift:], part[:, :per_far - shift]], axis=1)
         reply_ref[(g + FAR_FIRST[0] - FAR_FIRST[1]) % far] = part
 
 
-def finish_kernel(back_ref, slot_ref, off_ref, fac_ref, kelvin_ref, out_hbm, kelvin_hbm, out_ref, sems):
+def finish_kernel(back_ref, slot_ref, off_ref, fac_ref, kelvin_ref, out_hbm, kelvin_hbm, out_ref, flat_ref, sems):
     levels, rows, _ = off_ref.shape
     n = slot_ref.shape[1]
     blocks = n // LANES
     fields = rows // blocks
     near, cap, width = back_ref.shape
-    save_kelvin = pltpu.make_async_copy(kelvin_ref, kelvin_hbm, sems.at[0])
+    for t in range(blocks):
+        flat_ref[:, t * LANES:(t + 1) * LANES] = kelvin_ref[:, t]
+    save_kelvin = pltpu.make_async_copy(flat_ref, kelvin_hbm, sems.at[0])
     save_kelvin.start()
     per_far = near * cap
     far = width // WORDS
@@ -302,32 +326,29 @@
     like = lambda x: shape(x.shape, x.dtype)
     held = lambda x: pltpu.VMEM(x.shape, x.dtype)
     vmem, hbm = pltpu.VMEM, pltpu.HBM
-    offsets, factors, send, slot, share, flux, links, bottom, drift = call(
+    offsets, factors, send, slot, *cells = call(
         lambda *refs: columns_kernel(far, near, *refs),
         [
             like(profile),
             like(profile),
             shape((far, SENT, near * CAP), f32),
             shape((2, n), i32),
-            like(fractions),
-            like(flux),
-            like(links),
-            like(bottom),
-            like(drift),
+            *[shape((x.shape[0], n // LANES, LANES), f32) for x in (fractions, flux, links, bottom, drift)],
         ],
         hbm,
         [vmem] * 9,
-        [held(x) for x in (profile, coefficients, owner, fractions, flags)] + [pltpu.SemaphoreType.DMA((7 + 2 * INP,))],
+        [held(x) for x in (profile, coefficients, owner, fractions, flags, flux, links, bottom, drift)]
+        + [pltpu.SemaphoreType.DMA((7 + 2 * INP,))],
         profile, coefficients, owner, fractions, flags, flux, links, bottom, drift,
     )
     got = exchange_parcels(send, near, FAR_FIRST[0], NEAR_FIRST[0])
     kelvin, reply = call(
         cells_kernel,
-        [like(bottom), shape((far, ANSWERED, near * CAP), f32)],
+        [like(cells[0]), shape((far, ANSWERED, near * CAP), f32)],
         vmem,
         [vmem] * 2,
-        [],
-        got, share, flux, links, bottom, drift,
+        [pltpu.VMEM((ANSWERED * n // LANES, LANES), f32)],
+        got, *cells,
     )
     back = exchange_parcels(reply, near, FAR_FIRST[1], NEAR_FIRST[1])
     advanced, kelvin = call(
@@ -335,7 +356,7 @@
         [like(profile), like(bottom)],
         vmem,
         [hbm] * 2,
-        [held(profile), pltpu.SemaphoreType.DMA((1 + PIECES,))],
+        [held(profile), held(bottom), pltpu.SemaphoreType.DMA((1 + PIECES,))],
         back, slot, offsets, factors, kelvin,
     )
     return unblocked(advanced, fields), kelvin

time: 64.9 us -> 64.8 us (level)
  no operation moved by 1% of the time
where the time goes in v5:
time: 64.8 us; the launch traced here: 64.5 us
  blocking collectives  59.6 us (92%)
  Pallas kernels  3.99 us (6%)
  between operations  0.66 us (1%)
    all_to_all x2, blocking collectives, exchange_parcels(): lax.all_to_all(parcels, axes, 0, 0, axis_index_groups=far_groups, tiled=T...  35.9 us
    all_to_all x2, blocking collectives, exchange_parcels(): lax.all_to_all(parcels, axes, 0, 0, axis_index_groups=near_groups, tiled=...  23.7 us
    pallas_call x3, Pallas kernels, call(): pl.pallas_call(kernel, out_shape=out_shape, in_specs=[pl.BlockSpec(memory...  3.99 us

profile of v5, /device:TPU:1, one launch (start us, length us, event | category | flops | bytes accessed | tf_op | source)
XLA Modules:
  0.0 64.5 jit_solution(16704037237992926572)
XLA Ops:
  0.6 1.9 %shard_map.104 = (f32[32,32,128]{2,1,0:T(8,128)S(1)}, f32[32,32,128]{2,1,0:T(8,128)S(1)}, f32[16,5,128]{2,1,0:T(8,128)S(1)}, s32[2,1024]{1,0:T(2,128)S(1)}, f32[...) custom-call(f32[32,32,128]{2,1,0:T(8,128)} %bitcast.25, ...), custom_call_target="tpu_custom_call" | custom-call | tf_op jit(solution)/shard_map/pallas_call | solution.py:284
  2.5 22.2 %all_to_all.20 = f32[16,5,128]{2,1,0:T(8,128)S(1)} all-to-all(f32[16,5,128]{2,1,0:T(8,128)S(1)} %get-tuple-element.15), channel_id=1, replica_groups={{256,288,320,352,384,416,448,480,0,32,64,96,128,160,192,224},{257,289,3..., dimensions={0} | all-to-all | bytes 81920 | tf_op jit(solution)/shard_map/all_to_all | solution.py:301
  24.7 0.1 copy.13
  24.8 12.2 %all_to_all.21.got_ref = f32[32,4,128]{2,1,0:T(4,128)S(1)} all-to-all(f32[32,4,128]{2,1,0:T(4,128)S(1)} %bitcast.26), channel_id=1, replica_groups={{22,23,24,25,26,27,28,29,30,31,0,1,2,3,4,5,6,7,8,9,10,11,12,13,14,15,16..., dimensions={0} | all-to-all | bytes 131072 | tf_op jit(solution)/shard_map/all_to_all | solution.py:304
  37.1 0.9 %shard_map.105 = (f32[6,8,128]{2,1,0:T(8,128)S(1)}, f32[16,4,128]{2,1,0:T(4,128)S(1)}) custom-call(f32[32,4,128]{2,1,0:T(4,128)S(1)} %all_to_all.21.got_ref, f32[6,8,128]{2,1,0:T(8,128)S(1)} %get-tuple-element.16.share_ref, f32[6,8,128]{2,1,0:T(8,128)S(1)} %get-tuple-element.17.base_ref, f32[6,8,128]{2,1,0:T(8,128)S(1)} %get-tuple-element.18.link_ref, ...), custom_call_target="tpu_custom_call" | custom-call | tf_op jit(solution)/shard_map/pallas_call | solution.py:284
  38.0 13.7 %all_to_all.22 = f32[16,4,128]{2,1,0:T(4,128)S(1)} all-to-all(f32[16,4,128]{2,1,0:T(4,128)S(1)} %get-tuple-element.21), channel_id=1, replica_groups={{256,288,320,352,384,416,448,480,0,32,64,96,128,160,192,224},{257,289,3..., dimensions={0} | all-to-all | bytes 65536 | tf_op jit(solution)/shard_map/all_to_all | solution.py:301
  51.7 0.1 copy.14
  51.8 11.5 %all_to_all.23.back_ref = f32[32,4,128]{2,1,0:T(4,128)S(1)} all-to-all(f32[32,4,128]{2,1,0:T(4,128)S(1)} %bitcast.27), channel_id=1, replica_groups={{22,23,24,25,26,27,28,29,30,31,0,1,2,3,4,5,6,7,8,9,10,11,12,13,14,15,16..., dimensions={0} | all-to-all | bytes 131072 | tf_op jit(solution)/shard_map/all_to_all | solution.py:304
  63.3 1.1 %shard_map.106 = (f32[32,32,128]{2,1,0:T(8,128)}, f32[6,1024]{1,0:T(8,128)}) custom-call(f32[32,4,128]{2,1,0:T(4,128)S(1)} %all_to_all.23.back_ref, s32[2,1024]{1,0:T(2,128)S(1)} %get-tuple-element.22.slot_ref, f32[32,32,128]{2,1,0:T(8,128)S(1)} %get-tuple-element.23.off_ref, f32[32,32,128]{2,1,0:T(8,128)S(1)} %get-tuple-element.24.fac_ref, ...), custom_call_target="tpu_custom_call" | custom-call | tf_op jit(solution)/shard_map/pallas_call | solution.py:284
  (2 shorter events, 0.0 us)

commit v6 on v5

--- a/solution.py
+++ b/solution.py
@@ -7,7 +7,7 @@
 
 SWEEPS = 3
 FAR_FIRST = (8, 8)
-NEAR_FIRST = (22, 22)
+NEAR_FIRST = 22
 WORDS = 8
 SENT = 5
 ANSWERED = 4
@@ -105,7 +105,7 @@
             totals[j] += jnp.sum(same.astype(jnp.int32), axis=0, keepdims=True)
     per_far = near * CAP
     row = (owner // near + (far - FAR_FIRST[0])) % far
-    lane = (owner % near + (near - NEAR_FIRST[0])) % near * CAP + jnp.concatenate(totals, axis=1)
+    lane = (owner % near + (near - NEAR_FIRST)) % near * CAP + jnp.concatenate(totals, axis=1)
     slot_ref[0:1] = row
     slot_ref[1:2] = lane
     place = one_hot(lane, per_far)
@@ -182,8 +182,9 @@
 
 
 def cells_kernel(got_ref, share_ref, base_ref, link_ref, bottom_ref, drift_ref, kelvin_ref, reply_ref, answer_ref):
-    far = reply_ref.shape[0]
-    per_far = reply_ref.shape[2]
+    near, cap, width = got_ref.shape
+    per_far = near * cap
+    far = width // WORDS
     kinds, blocks, _ = share_ref.shape
     got = got_ref[...].reshape(per_far, far * WORDS).T
     high = got.astype(jnp.bfloat16).astype(jnp.float32)
@@ -233,13 +234,11 @@
     reply = jnp.zeros((two, far * per_far), jnp.float32)
     for b in range(0, blocks, 2):
         reply = reply + jnp.where(first == block - b, spread[b * ANSWERED:b * ANSWERED + two], 0.0)
-    reply = reply[:ANSWERED] + reply[ANSWERED:]
-    shift = (NEAR_FIRST[0] - NEAR_FIRST[1]) * CAP % per_far
-    for g in range(far):
-        part = reply[:, g * per_far:(g + 1) * per_far]
-        if shift:
-            part = jnp.concatenate([part[:, per_far - shift:], part[:, :per_far - shift]], axis=1)
-        reply_ref[(g + FAR_FIRST[0] - FAR_FIRST[1]) % far] = part
+    reply = reply + jnp.concatenate([reply[ANSWERED:], reply[:ANSWERED]], axis=0)
+    turn = FAR_FIRST[1] - FAR_FIRST[0]
+    order = [(g + turn) % far for g in range(far)]
+    reply = jnp.concatenate([reply[:, g * per_far:(g + 1) * per_far] for g in order], axis=0)
+    reply_ref[...] = reply.T.reshape(reply_ref.shape)
 
 
 def finish_kernel(back_ref, slot_ref, off_ref, fac_ref, kelvin_ref, out_hbm, kelvin_hbm, out_ref, flat_ref, sems):
@@ -247,21 +246,20 @@
     n = slot_ref.shape[1]
     blocks = n // LANES
     fields = rows // blocks
-    near, cap, width = back_ref.shape
+    far = back_ref.shape[0] // ANSWERED
     for t in range(blocks):
         flat_ref[:, t * LANES:(t + 1) * LANES] = kelvin_ref[:, t]
     save_kelvin = pltpu.make_async_copy(flat_ref, kelvin_hbm, sems.at[0])
     save_kelvin.start()
-    per_far = near * cap
-    far = width // WORDS
     row = (slot_ref[0:1] + (far + FAR_FIRST[0] - FAR_FIRST[1])) % far
-    shift = (NEAR_FIRST[0] - NEAR_FIRST[1]) * CAP % per_far
-    place = one_hot((slot_ref[1:2] + shift) % per_far, per_far)
-    back = back_ref[...].reshape(per_far, width).T
-    spread = dot(jnp.concatenate(halves(back), axis=1), jnp.concatenate([place, place], axis=0), NN)
-    level = jnp.zeros((WORDS, n), jnp.float32)
-    for g in range(far):
-        level = level + jnp.where(row == g, spread[g * WORDS:(g + 1) * WORDS], 0.0)
+    place = one_hot(slot_ref[1:2], LANES)
+    spread = dot(jnp.concatenate(halves(back_ref[...]), axis=1), jnp.concatenate([place, place], axis=0), NN)
+    two = 2 * ANSWERED
+    first = lax.broadcasted_iota(jnp.int32, (two, n), 0) // ANSWERED
+    level = jnp.zeros((two, n), jnp.float32)
+    for g in range(0, far, 2):
+        level = level + jnp.where(first == row - g, spread[g * ANSWERED:g * ANSWERED + two], 0.0)
+    level = level[:ANSWERED] + level[ANSWERED:]
     level = jnp.concatenate([level[0:fields, t * LANES:(t + 1) * LANES] for t in range(blocks)], axis=0)
     saves = []
     step = levels // PIECES
@@ -291,17 +289,33 @@
     )(*args)
 
 
-def exchange_parcels(parcels, near, far_first, near_first):
+def groups_of(far, near, far_first):
+    far_order = [(k + far_first) % far for k in range(far)]
+    near_order = [(k + NEAR_FIRST) % near for k in range(near)]
+    return (
+        [[f * near + q for f in far_order] for q in range(near)],
+        [[f * near + q for q in near_order] for f in range(far)],
+    )
+
+
+def swap(parcels, groups):
+    return lax.all_to_all(parcels, ("gx", "gy", "sa"), 0, 0, axis_index_groups=groups, tiled=True)
+
+
+def send_to_cells(parcels, near):
     far, words, _ = parcels.shape
-    axes = ("gx", "gy", "sa")
-    far_order = [(k + far_first) % far for k in range(far)]
-    near_order = [(k + near_first) % near for k in range(near)]
-    far_groups = [[f * near + q for f in far_order] for q in range(near)]
-    near_groups = [[f * near + q for q in near_order] for f in range(far)]
-    parcels = lax.all_to_all(parcels, axes, 0, 0, axis_index_groups=far_groups, tiled=True)
-    parcels = jnp.pad(parcels, ((0, 0), (0, WORDS - words), (0, 0)))
+    far_groups, near_groups = groups_of(far, near, FAR_FIRST[0])
+    parcels = jnp.pad(swap(parcels, far_groups), ((0, 0), (0, WORDS - words), (0, 0)))
     parcels = parcels.reshape(far * WORDS, near * CAP).T.reshape(near, CAP, far * WORDS)
-    return lax.all_to_all(parcels, axes, 0, 0, axis_index_groups=near_groups, tiled=True)
+    return swap(parcels, near_groups)
+
+
+def send_back(parcels):
+    near, cap, width = parcels.shape
+    far = width // WORDS
+    far_groups, near_groups = groups_of(far, near, FAR_FIRST[1])
+    parcels = swap(parcels, near_groups).reshape(near * cap, width).T.reshape(far, WORDS, near * cap)
+    return swap(parcels[:, :ANSWERED], far_groups).reshape(far * ANSWERED, near * cap)
 
 
 def blocked(x):
@@ -341,16 +355,16 @@
         + [pltpu.SemaphoreType.DMA((7 + 2 * INP,))],
         profile, coefficients, owner, fractions, flags, flux, links, bottom, drift,
     )
-    got = exchange_parcels(send, near, FAR_FIRST[0], NEAR_FIRST[0])
+    got = send_to_cells(send, near)
     kelvin, reply = call(
         cells_kernel,
-        [like(cells[0]), shape((far, ANSWERED, near * CAP), f32)],
+        [like(cells[0]), like(got)],
         vmem,
         [vmem] * 2,
         [pltpu.VMEM((ANSWERED * n // LANES, LANES), f32)],
         got, *cells,
     )
-    back = exchange_parcels(reply, near, FAR_FIRST[1], NEAR_FIRST[1])
+    back = send_back(reply)
     advanced, kelvin = call(
         finish_kernel,
         [like(profile), like(bottom)],

time: 64.8 us -> 63.8 us (0.985)
  blocking collectives: 59.6 us -> 58.5 us
    all_to_all x4, blocking collectives: 59.6 us -> 58.5 us  [swap(): lax.all_to_all(parcels, ('gx', 'gy', 'sa'), 0, 0, axis_index_groups=group...]
where the time goes in v6:
time: 63.8 us; the launch traced here: 63.4 us
  blocking collectives  58.5 us (92%)
  Pallas kernels  4.02 us (6%)
  between operations  0.68 us (1%)
    all_to_all x4, blocking collectives, swap(): lax.all_to_all(parcels, ('gx', 'gy', 'sa'), 0, 0, axis_index_groups=group...  58.5 us
    pallas_call x3, Pallas kernels, call(): pl.pallas_call(kernel, out_shape=out_shape, in_specs=[pl.BlockSpec(memory...  4.02 us

profile of v6, /device:TPU:1, one launch (start us, length us, event | category | flops | bytes accessed | tf_op | source)
XLA Modules:
  0.0 63.4 jit_solution(4918936421869401828)
XLA Ops:
  0.6 1.9 %shard_map.104 = (f32[32,32,128]{2,1,0:T(8,128)S(1)}, f32[32,32,128]{2,1,0:T(8,128)S(1)}, f32[16,5,128]{2,1,0:T(8,128)S(1)}, s32[2,1024]{1,0:T(2,128)S(1)}, f32[...) custom-call(f32[32,32,128]{2,1,0:T(8,128)} %bitcast.26, ...), custom_call_target="tpu_custom_call" | custom-call | tf_op jit(solution)/shard_map/pallas_call | solution.py:282
  2.5 22.2 %all_to_all.20 = f32[16,5,128]{2,1,0:T(8,128)S(1)} all-to-all(f32[16,5,128]{2,1,0:T(8,128)S(1)} %get-tuple-element.15), channel_id=1, replica_groups={{256,288,320,352,384,416,448,480,0,32,64,96,128,160,192,224},{257,289,3..., dimensions={0} | all-to-all | bytes 81920 | tf_op jit(solution)/shard_map/all_to_all | solution.py:302
  24.7 0.1 copy.13
  24.8 12.2 %all_to_all.21.got_ref = f32[32,4,128]{2,1,0:T(4,128)S(1)} all-to-all(f32[32,4,128]{2,1,0:T(4,128)S(1)} %bitcast.27), channel_id=1, replica_groups={{22,23,24,25,26,27,28,29,30,31,0,1,2,3,4,5,6,7,8,9,10,11,12,13,14,15,16..., dimensions={0} | all-to-all | bytes 131072 | tf_op jit(solution)/shard_map/all_to_all | solution.py:302
  37.1 1.0 %shard_map.105 = (f32[6,8,128]{2,1,0:T(8,128)S(1)}, f32[32,4,128]{2,1,0:T(4,128)S(1)}) custom-call(f32[32,4,128]{2,1,0:T(4,128)S(1)} %all_to_all.21.got_ref, f32[6,8,128]{2,1,0:T(8,128)S(1)} %get-tuple-element.16.share_ref, f32[6,8,128]{2,1,0:T(8,128)S(1)} %get-tuple-element.17.base_ref, f32[6,8,128]{2,1,0:T(8,128)S(1)} %get-tuple-element.18.link_ref, ...), custom_call_target="tpu_custom_call" | custom-call | tf_op jit(solution)/shard_map/pallas_call | solution.py:282
  38.1 10.4 %all_to_all.22 = f32[32,4,128]{2,1,0:T(4,128)S(1)} all-to-all(f32[32,4,128]{2,1,0:T(4,128)S(1)} %get-tuple-element.21), channel_id=1, replica_groups={{22,23,24,25,26,27,28,29,30,31,0,1,2,3,4,5,6,7,8,9,10,11,12,13,14,15,16..., dimensions={0} | all-to-all | bytes 131072 | tf_op jit(solution)/shard_map/all_to_all | solution.py:302
  48.5 0.1 copy.14
  48.6 13.7 %all_to_all.23 = f32[16,4,128]{2,1,0:T(4,128)S(1)} all-to-all(f32[16,4,128]{2,1,0:T(4,128)S(1)} %slice.4), channel_id=1, replica_groups={{256,288,320,352,384,416,448,480,0,32,64,96,128,160,192,224},{257,289,3..., dimensions={0} | all-to-all | bytes 65536 | tf_op jit(solution)/shard_map/all_to_all | solution.py:302
  62.3 1.1 %shard_map.106 = (f32[32,32,128]{2,1,0:T(8,128)}, f32[6,1024]{1,0:T(8,128)}) custom-call(f32[64,128]{1,0:T(8,128)S(1)} %bitcast.25, s32[2,1024]{1,0:T(2,128)S(1)} %get-tuple-element.22.slot_ref, f32[32,32,128]{2,1,0:T(8,128)S(1)} %get-tuple-element.23.off_ref, f32[32,32,128]{2,1,0:T(8,128)S(1)} %get-tuple-element.24.fac_ref, ...), custom_call_target="tpu_custom_call" | custom-call | tf_op jit(solution)/shard_map/pallas_call | solution.py:282
  (2 shorter events, 0.0 us)

commit v7 on v6

--- a/solution.py
+++ b/solution.py
@@ -6,7 +6,7 @@
 from jax.sharding import PartitionSpec as P
 
 SWEEPS = 3
-FAR_FIRST = (8, 8)
+FAR_FIRST = (10, 10)
 NEAR_FIRST = 22
 WORDS = 8
 SENT = 5
@@ -157,7 +157,9 @@
     sent = dot(spread, place, NT)
     for g in range(far):
         at = 2 * g * WORDS
-        send_ref[g] = sent[at:at + SENT] + sent[at + WORDS:at + WORDS + SENT]
+        both = sent[at:at + SENT] + sent[at + WORDS:at + WORDS + SENT]
+        for w in range(SENT):
+            send_ref[g, w] = both[w:w + 1]
 
     rest = copies[1 + 2 * INP:]
     rest[0].wait()
@@ -303,9 +305,9 @@
 
 
 def send_to_cells(parcels, near):
-    far, words, _ = parcels.shape
+    far, words = parcels.shape[:2]
     far_groups, near_groups = groups_of(far, near, FAR_FIRST[0])
-    parcels = jnp.pad(swap(parcels, far_groups), ((0, 0), (0, WORDS - words), (0, 0)))
+    parcels = jnp.pad(swap(parcels, far_groups).reshape(far, words, near * CAP), ((0, 0), (0, WORDS - words), (0, 0)))
     parcels = parcels.reshape(far * WORDS, near * CAP).T.reshape(near, CAP, far * WORDS)
     return swap(parcels, near_groups)
 
@@ -345,7 +347,7 @@
         [
             like(profile),
             like(profile),
-            shape((far, SENT, near * CAP), f32),
+            shape((far, SENT, 1, near * CAP), f32),
             shape((2, n), i32),
             *[shape((x.shape[0], n // LANES, LANES), f32) for x in (fractions, flux, links, bottom, drift)],
         ],

time: 63.8 us -> 63.5 us (level)
  no operation moved by 1% of the time
where the time goes in v7:
time: 63.5 us; the launch traced here: 63.2 us
  blocking collectives  58.3 us (92%)
  Pallas kernels  4.02 us (6%)
  between operations  0.68 us (1%)
    all_to_all x4, blocking collectives, swap(): lax.all_to_all(parcels, ('gx', 'gy', 'sa'), 0, 0, axis_index_groups=group...  58.3 us
    pallas_call x3, Pallas kernels, call(): pl.pallas_call(kernel, out_shape=out_shape, in_specs=[pl.BlockSpec(memory...  4.02 us

profile of v7, /device:TPU:1, one launch (start us, length us, event | category | flops | bytes accessed | tf_op | source)
XLA Modules:
  0.0 63.2 jit_solution(12219849480957589555)
XLA Ops:
  0.6 1.9 %shard_map.104 = (f32[32,32,128]{2,1,0:T(8,128)S(1)}, f32[32,32,128]{2,1,0:T(8,128)S(1)}, f32[16,5,1,128]{3,2,1,0:T(1,128)S(1)}, s32[2,1024]{1,0:T(2,128)S(1)}, ...) custom-call(f32[32,32,128]{2,1,0:T(8,128)} %bitcast.30, ...), custom_call_target="tpu_custom_call" | custom-call | tf_op jit(solution)/shard_map/pallas_call | solution.py:284
  2.5 21.5 %all_to_all.20 = f32[16,5,1,128]{3,2,1,0:T(1,128)S(1)} all-to-all(f32[16,5,1,128]{3,2,1,0:T(1,128)S(1)} %get-tuple-element.15), channel_id=1, replica_groups={{320,352,384,416,448,480,0,32,64,96,128,160,192,224,256,288},{321,353,3..., dimensions={0} | all-to-all | bytes 81920 | tf_op jit(solution)/shard_map/all_to_all | solution.py:304
  24.0 0.1 copy.25
  24.1 12.4 %all_to_all.21.got_ref = f32[32,4,128]{2,1,0:T(4,128)S(1)} all-to-all(f32[32,4,128]{2,1,0:T(4,128)S(1)} %bitcast.31), channel_id=1, replica_groups={{22,23,24,25,26,27,28,29,30,31,0,1,2,3,4,5,6,7,8,9,10,11,12,13,14,15,16..., dimensions={0} | all-to-all | bytes 131072 | tf_op jit(solution)/shard_map/all_to_all | solution.py:304
  36.5 1.0 %shard_map.105 = (f32[6,8,128]{2,1,0:T(8,128)S(1)}, f32[32,4,128]{2,1,0:T(4,128)S(1)}) custom-call(f32[32,4,128]{2,1,0:T(4,128)S(1)} %all_to_all.21.got_ref, f32[6,8,128]{2,1,0:T(8,128)S(1)} %get-tuple-element.16.share_ref, f32[6,8,128]{2,1,0:T(8,128)S(1)} %get-tuple-element.17.base_ref, f32[6,8,128]{2,1,0:T(8,128)S(1)} %get-tuple-element.18.link_ref, ...), custom_call_target="tpu_custom_call" | custom-call | tf_op jit(solution)/shard_map/pallas_call | solution.py:284
  37.6 10.4 %all_to_all.22 = f32[32,4,128]{2,1,0:T(4,128)S(1)} all-to-all(f32[32,4,128]{2,1,0:T(4,128)S(1)} %get-tuple-element.21), channel_id=1, replica_groups={{22,23,24,25,26,27,28,29,30,31,0,1,2,3,4,5,6,7,8,9,10,11,12,13,14,15,16..., dimensions={0} | all-to-all | bytes 131072 | tf_op jit(solution)/shard_map/all_to_all | solution.py:304
  47.9 0.1 copy.26
  48.0 14.1 %all_to_all.23 = f32[16,4,128]{2,1,0:T(4,128)S(1)} all-to-all(f32[16,4,128]{2,1,0:T(4,128)S(1)} %slice.4), channel_id=1, replica_groups={{320,352,384,416,448,480,0,32,64,96,128,160,192,224,256,288},{321,353,3..., dimensions={0} | all-to-all | bytes 65536 | tf_op jit(solution)/shard_map/all_to_all | solution.py:304
  62.1 1.1 %shard_map.106 = (f32[32,32,128]{2,1,0:T(8,128)}, f32[6,1024]{1,0:T(8,128)}) custom-call(f32[64,128]{1,0:T(8,128)S(1)} %bitcast.29, s32[2,1024]{1,0:T(2,128)S(1)} %get-tuple-element.22.slot_ref, f32[32,32,128]{2,1,0:T(8,128)S(1)} %get-tuple-element.23.off_ref, f32[32,32,128]{2,1,0:T(8,128)S(1)} %get-tuple-element.24.fac_ref, ...), custom_call_target="tpu_custom_call" | custom-call | tf_op jit(solution)/shard_map/pallas_call | solution.py:284
  (3 shorter events, 0.0 us)

commit v8 on v7

--- a/solution.py
+++ b/solution.py
@@ -6,7 +6,7 @@
 from jax.sharding import PartitionSpec as P
 
 SWEEPS = 3
-FAR_FIRST = (10, 10)
+FAR_FIRST = (10, 9)
 NEAR_FIRST = 22
 WORDS = 8
 SENT = 5

time: 63.5 us -> 63.3 us (level)
  no operation moved by 1% of the time
where the time goes in v8:
time: 63.3 us; the launch traced here: 63 us
  blocking collectives  58.1 us (92%)
  Pallas kernels  4.05 us (6%)
  between operations  0.68 us (1%)
    all_to_all x4, blocking collectives, swap(): lax.all_to_all(parcels, ('gx', 'gy', 'sa'), 0, 0, axis_index_groups=group...  58.1 us
    pallas_call x3, Pallas kernels, call(): pl.pallas_call(kernel, out_shape=out_shape, in_specs=[pl.BlockSpec(memory...  4.05 us

profile of v8, /device:TPU:1, one launch (start us, length us, event | category | flops | bytes accessed | tf_op | source)
XLA Modules:
  0.0 63.0 jit_solution(4908078209259422872)
XLA Ops:
  0.6 1.9 %shard_map.104 = (f32[32,32,128]{2,1,0:T(8,128)S(1)}, f32[32,32,128]{2,1,0:T(8,128)S(1)}, f32[16,5,1,128]{3,2,1,0:T(1,128)S(1)}, s32[2,1024]{1,0:T(2,128)S(1)}, ...) custom-call(f32[32,32,128]{2,1,0:T(8,128)} %bitcast.30, ...), custom_call_target="tpu_custom_call" | custom-call | tf_op jit(solution)/shard_map/pallas_call | solution.py:284
  2.5 21.5 %all_to_all.20 = f32[16,5,1,128]{3,2,1,0:T(1,128)S(1)} all-to-all(f32[16,5,1,128]{3,2,1,0:T(1,128)S(1)} %get-tuple-element.15), channel_id=1, replica_groups={{320,352,384,416,448,480,0,32,64,96,128,160,192,224,256,288},{321,353,3..., dimensions={0} | all-to-all | bytes 81920 | tf_op jit(solution)/shard_map/all_to_all | solution.py:304
  24.0 0.1 copy.25
  24.1 12.4 %all_to_all.21.got_ref = f32[32,4,128]{2,1,0:T(4,128)S(1)} all-to-all(f32[32,4,128]{2,1,0:T(4,128)S(1)} %bitcast.31), channel_id=1, replica_groups={{22,23,24,25,26,27,28,29,30,31,0,1,2,3,4,5,6,7,8,9,10,11,12,13,14,15,16..., dimensions={0} | all-to-all | bytes 131072 | tf_op jit(solution)/shard_map/all_to_all | solution.py:304
  36.5 1.1 %shard_map.105 = (f32[6,8,128]{2,1,0:T(8,128)S(1)}, f32[32,4,128]{2,1,0:T(4,128)S(1)}) custom-call(f32[32,4,128]{2,1,0:T(4,128)S(1)} %all_to_all.21.got_ref, f32[6,8,128]{2,1,0:T(8,128)S(1)} %get-tuple-element.16.share_ref, f32[6,8,128]{2,1,0:T(8,128)S(1)} %get-tuple-element.17.base_ref, f32[6,8,128]{2,1,0:T(8,128)S(1)} %get-tuple-element.18.link_ref, ...), custom_call_target="tpu_custom_call" | custom-call | tf_op jit(solution)/shard_map/pallas_call | solution.py:284
  37.6 10.4 %all_to_all.22 = f32[32,4,128]{2,1,0:T(4,128)S(1)} all-to-all(f32[32,4,128]{2,1,0:T(4,128)S(1)} %get-tuple-element.21), channel_id=1, replica_groups={{22,23,24,25,26,27,28,29,30,31,0,1,2,3,4,5,6,7,8,9,10,11,12,13,14,15,16..., dimensions={0} | all-to-all | bytes 131072 | tf_op jit(solution)/shard_map/all_to_all | solution.py:304
  47.9 0.1 copy.26
  48.1 13.8 %all_to_all.23 = f32[16,4,128]{2,1,0:T(4,128)S(1)} all-to-all(f32[16,4,128]{2,1,0:T(4,128)S(1)} %slice.4), channel_id=1, replica_groups={{288,320,352,384,416,448,480,0,32,64,96,128,160,192,224,256},{289,321,3..., dimensions={0} | all-to-all | bytes 65536 | tf_op jit(solution)/shard_map/all_to_all | solution.py:304
  61.9 1.1 %shard_map.106 = (f32[32,32,128]{2,1,0:T(8,128)}, f32[6,1024]{1,0:T(8,128)}) custom-call(f32[64,128]{1,0:T(8,128)S(1)} %bitcast.29, s32[2,1024]{1,0:T(2,128)S(1)} %get-tuple-element.22.slot_ref, f32[32,32,128]{2,1,0:T(8,128)S(1)} %get-tuple-element.23.off_ref, f32[32,32,128]{2,1,0:T(8,128)S(1)} %get-tuple-element.24.fac_ref, ...), custom_call_target="tpu_custom_call" | custom-call | tf_op jit(solution)/shard_map/pallas_call | solution.py:284
  (3 shorter events, 0.0 us)
